TPU v7x, 128 devices: a whole 4x4x4 slice. The times are simulated.
128 devices in a mesh: space: 32 (over z, x, core), head: 4 (over y).
Axes of the slice: x: 4, y: 4, z: 4, core: 2. Of those that a mesh axis runs over, the one named last changes fastest.
Arguments:
- tokens: bfloat16 [32768, 1024], P('space'), may hold values from -70 to 70
- w_qkv: bfloat16 [1024, 3, 1024], P(None, None, 'head'), may hold values from -7 to 7
- w_out: bfloat16 [1024, 1024], P('head'), may hold values from -0.5 to 0.5
- neighbours: int32 [256, 9], P('space'), may hold values from 0 to 71, as said below
- requests: int32 [32, 32, 2], P('space'), may hold values from -1 to 7, as said below
- cotangent: bfloat16 [32768, 1024], P('space', 'head'), may hold values from -6 to 6
Outputs:
- layer_out: bfloat16 [32768, 1024], P('space', 'head')
- grad_tokens: bfloat16 [32768, 1024], P('space', 'head')
- grad_w_qkv: float32 [1024, 3, 1024], P('space', None, 'head')
- grad_w_out: float32 [1024, 1024], P('head', 'space')
Inputs may be any that keep to these rules, and one draw needn't show every extreme that they name: `neighbours`: row t starts with t % 8 itself, then 3 other tiles of the same device, then 5 slot entries 8 + p * 2 + c; every slot entry names a filled request of that device, every filled request is named by some tile of that device, and no row names a tile twice. requests[d, p, c] is a tile of device p by its index within p, or -1 for an empty slot; filled slots come first and are distinct, requests[d, d] is empty, and in every draw some device fills all 2 slots towards some other device.
All inputs are finite; a program needn't handle non-finite values.
Results may differ from a plain program's by a relative error of at most 0.02.
The roundings to bfloat16 on the way count: a program that leaves them out, or rounds other values in their place, can miss the bound.
Values may be sent and summed in bfloat16 or wider, within the bound.
A program may use at most 192 MiB of HBM per device.

v0:
```python
import jax
import jax.numpy as jnp
from jax import lax
from jax.sharding import PartitionSpec as P

HEAD_DIM = 64
BLOCK_TILES = 4
NEIGHBOURS = 9


EPSILON = 1e-05


def norm_parts(tokens):
    values = tokens.astype(jnp.float32)
    centred = values - jnp.mean(values, axis=1, keepdims=True)
    inverse = lax.rsqrt(jnp.mean(centred * centred, axis=1, keepdims=True) + EPSILON)
    return (centred * inverse, inverse)


def gather_keys(extended, block_entries, head_count):
    entry_count = block_entries.shape[0]
    tile_rows = extended.shape[2]
    picked = jnp.take(extended, block_entries.reshape(-1), axis=1)
    return picked.reshape(2, entry_count, NEIGHBOURS * tile_rows, head_count, HEAD_DIM)


def probabilities(queries, key_part, score_scale):
    scores = (
        jnp.einsum("bihe,bjhe->bhij", queries, key_part, preferred_element_type=jnp.float32)
        * score_scale
    )
    row_top = jnp.max(scores, axis=3, keepdims=True)
    weights = jnp.exp(scores - row_top)
    return weights / jnp.sum(weights, axis=3, keepdims=True)


def select_pairs(local_pairs, incoming):
    peer_count, slot_count = incoming.shape
    flat_wanted = incoming.reshape(-1)
    usable = (flat_wanted >= 0)[None, :, None, None]
    picked = jnp.take(local_pairs, jnp.maximum(flat_wanted, 0), axis=1)
    picked = jnp.where(usable, picked, jnp.zeros_like(picked))
    return picked.reshape(2, peer_count, slot_count, local_pairs.shape[2], local_pairs.shape[3])


def on_device(tokens, w_qkv, w_out, neighbours, requests, cotangent):
    row_count, model_width = tokens.shape
    tile_count = neighbours.shape[0]
    tile_rows = row_count // tile_count
    head_width = w_qkv.shape[2]
    head_count = head_width // HEAD_DIM
    peer_count = lax.axis_size("space")
    slot_count = requests.shape[2]
    col_share = cotangent.shape[1]
    column = lax.axis_index("head") * col_share
    score_scale = HEAD_DIM ** (-0.5)
    block_count = tile_count // BLOCK_TILES
    extent = tile_count + peer_count * slot_count
    standard, inverse = norm_parts(tokens)
    normed = standard.astype(jnp.bfloat16)
    flat_weight = w_qkv.reshape(model_width, 3 * head_width)
    projected = jnp.dot(normed, flat_weight, preferred_element_type=jnp.float32).astype(
        jnp.bfloat16
    )
    queries = projected[:, :head_width].reshape(
        block_count, BLOCK_TILES, tile_rows, head_count, HEAD_DIM
    )
    local_pairs = jnp.transpose(
        projected[:, head_width:].reshape(row_count, 2, head_width), (1, 0, 2)
    )
    local_pairs = local_pairs.reshape(2, tile_count, tile_rows, head_width)
    entries = neighbours.reshape(block_count, BLOCK_TILES, NEIGHBOURS)
    incoming = lax.all_to_all(
        requests.reshape(peer_count, slot_count), "space", split_axis=0, concat_axis=0, tiled=True
    )
    outgoing = select_pairs(local_pairs, incoming)
    fetched, incoming = (
        lax.all_to_all(outgoing, "space", split_axis=1, concat_axis=1, tiled=True),
        incoming,
    )
    extended = jnp.concatenate(
        [local_pairs, fetched.reshape(2, peer_count * slot_count, tile_rows, head_width)], 1
    )

    def forward_block(inputs):
        block_queries, block_entries = inputs
        keyset = gather_keys(extended, block_entries, head_count)
        likely = probabilities(block_queries, keyset[0], score_scale)
        rounded = likely.astype(jnp.bfloat16)
        mixed = jnp.einsum(
            "bhij,bjhe->bihe", rounded, keyset[1], preferred_element_type=jnp.float32
        )
        return mixed.astype(jnp.bfloat16)

    attended = lax.map(forward_block, (queries, entries)).reshape(row_count, head_width)
    partial_out = jnp.dot(attended, w_out, preferred_element_type=jnp.float32)
    summed = lax.psum_scatter(
        partial_out.astype(jnp.bfloat16), "head", scatter_dimension=1, tiled=True
    ).astype(jnp.float32)
    own_tokens = lax.dynamic_slice_in_dim(tokens, column, col_share, 1).astype(jnp.float32)
    layer_out = (own_tokens + summed).astype(jnp.bfloat16)
    cotangent_full = lax.all_gather(cotangent, "head", axis=1, tiled=True)
    grad_attended = jnp.einsum(
        "td,fd->tf", cotangent_full, w_out, preferred_element_type=jnp.float32
    ).astype(jnp.bfloat16)
    grad_blocks = grad_attended.reshape(block_count, BLOCK_TILES, tile_rows, head_count, HEAD_DIM)
    resent = lax.all_to_all(
        select_pairs(local_pairs, incoming), "space", split_axis=1, concat_axis=1, tiled=True
    )
    backward_keys = jnp.concatenate(
        [local_pairs, resent.reshape(2, peer_count * slot_count, tile_rows, head_width)], 1
    )

    def backward_block(totals, triple):
        block_queries, block_entries, block_grads = triple
        keyset = gather_keys(backward_keys, block_entries, head_count)
        key_part = keyset[0]
        value_part = keyset[1]
        likely = probabilities(block_queries, key_part, score_scale)
        rounded = likely.astype(jnp.bfloat16)
        grad_prob = jnp.einsum(
            "bihe,bjhe->bhij", block_grads, value_part, preferred_element_type=jnp.float32
        )
        row_delta = jnp.sum(likely * grad_prob, axis=3, keepdims=True)
        grad_score = (likely * (grad_prob - row_delta) * score_scale).astype(jnp.bfloat16)
        grad_query = jnp.einsum(
            "bhij,bjhe->bihe", grad_score, key_part, preferred_element_type=jnp.float32
        )
        grad_key = jnp.einsum(
            "bhij,bihe->bjhe", grad_score, block_queries, preferred_element_type=jnp.float32
        )
        grad_value = jnp.einsum(
            "bhij,bihe->bjhe", rounded, block_grads, preferred_element_type=jnp.float32
        )
        entry_count = block_entries.shape[0] * NEIGHBOURS
        flat_entries = block_entries.reshape(-1)
        both_grads = jnp.stack(
            [grad_key.reshape(entry_count, -1), grad_value.reshape(entry_count, -1)], 0
        )
        return (totals.at[:, flat_entries].add(both_grads), grad_query)

    empty_total = jnp.zeros((2, extent, tile_rows * head_width), jnp.float32)
    pair_totals, query_grads = lax.scan(
        backward_block, empty_total, (queries, entries, grad_blocks)
    )
    near_part = pair_totals[:, :tile_count]
    far_part = (
        pair_totals[:, tile_count:]
        .astype(jnp.bfloat16)
        .reshape(2, peer_count, slot_count, tile_rows, head_width)
    )
    returned = lax.all_to_all(far_part, "space", split_axis=1, concat_axis=1, tiled=True)
    placer = (jnp.arange(tile_count, dtype=jnp.int32)[:, None] == incoming.reshape(1, -1)).astype(
        jnp.float32
    )
    landed = jnp.einsum(
        "tp,gpx->gtx",
        placer,
        returned.reshape(2, peer_count * slot_count, -1).astype(jnp.float32),
        precision=lax.Precision.HIGHEST,
    )
    pair_grads = (near_part + landed).reshape(2, row_count, head_width)
    grad_qkv = jnp.concatenate(
        [query_grads.reshape(1, row_count, head_width), pair_grads], 0
    ).astype(jnp.bfloat16)
    normed_rows = normed.T
    cotangent_rows = cotangent_full.T
    input_part = jnp.einsum(
        "ct,gtf->cgf", normed_rows, grad_qkv, preferred_element_type=jnp.float32
    )
    output_part = jnp.dot(cotangent_rows, attended, preferred_element_type=jnp.float32)
    stacked_grads = lax.psum_scatter(
        jnp.concatenate(
            [
                input_part.reshape(
                    model_width // peer_count * lax.axis_size("space"), 3 * head_width
                ),
                output_part,
            ],
            1,
        ).astype(jnp.bfloat16),
        "space",
        scatter_dimension=0,
        tiled=True,
    ).astype(jnp.float32)
    grad_w_qkv = stacked_grads[:, : 3 * head_width].reshape(-1, 3, head_width)
    grad_w_out = stacked_grads[:, 3 * head_width :].T
    grad_normed = jnp.einsum("gtf,dgf->td", grad_qkv, w_qkv, preferred_element_type=jnp.float32)
    own_standard = lax.dynamic_slice_in_dim(standard, column, col_share, 1)
    own_part = lax.psum_scatter(
        grad_normed.astype(jnp.bfloat16), "head", scatter_dimension=1, tiled=True
    ).astype(jnp.float32)
    row_sums = lax.psum(
        (jnp.sum(own_part, axis=1), jnp.sum(own_part * own_standard, axis=1)), "head"
    )
    first_mean = (row_sums[0] / model_width)[:, None]
    second_mean = (row_sums[1] / model_width)[:, None]
    cotangent_wide = cotangent.astype(jnp.float32)
    grad_tokens = (
        cotangent_wide + inverse * (own_part - first_mean - own_standard * second_mean)
    ).astype(jnp.bfloat16)
    return (layer_out, grad_tokens, grad_w_qkv, grad_w_out)


def solution(mesh):
    placed = (
        P("space", None),
        P(None, None, "head"),
        P("head", None),
        P("space", None),
        P("space", None, None),
        P("space", "head"),
    )
    return jax.shard_map(
        on_device,
        mesh=mesh,
        in_specs=placed,
        out_specs=(
            P("space", "head"),
            P("space", "head"),
            P("space", None, "head"),
            P("head", "space"),
        ),
        check_vma=False,
    )
```

profile of v0, /device:TPU:1, one launch (start us, length us, event | category | flops | bytes accessed | tf_op | source)
XLA Modules:
  0.0 915.5 jit_solution(7193930980082506994)
XLA Ops:
  8.7 9.4 %all-to-all-start = ((s32[32,1,2]{2,1,0:T(1,128)}), s32[32,1,2]{2,1,0:T(1,128)S(1)}, u32[]{:S(2)}, u32[]{:S(2)}) async-start(s32[32,1,2]{2,1,0:T(1,128)} %copy.125), calls=%async_computation | async-start | bytes 32768 | tf_op jit(solution)/shard_map/all_to_all | solution.py:74
  31.5 5.3 gather_fusion.2
  36.8 7.6 bitcast_select_fusion
  44.4 7.7 copy.127
  52.1 7.5 all-to-all-start.1
  61.7 35.3 %all-gather.2.cloned.1.call-done = bf16[1024,1024]{1,0:T(8,128)(2,1)} async-done(((bf16[1024,256]{1,0:T(8,128)(2,1)}), bf16[1024,1024]{1,0:T(8,128)(2,1)}) %all-gather.2.cloned.1.call-update) | async-done | bytes 2097168 | tf_op jit(solution)/shard_map/all_gather | solution.py:103
  100.3 59.1 %all-to-all-done.1 = bf16[2,32,2,128,256]{4,3,2,0,1:T(8,128)(2,1)} async-done(((bf16[2,32,2,128,256]{4,3,2,0,1:T(8,128)(2,1)}), bf16[2,32,2,128,256]{4,3,2,0,1:T(8,128)(2,1)}, u32[]{:S(2)}, u32[]{:S(2)}) %all-to-all-start.1) | async-done | bytes 8388640 | tf_op jit(solution)/shard_map/all_to_all | solution.py:79
  159.4 7.8 copy.128
  167.2 7.8 pad_maximum_fusion
  175.0 6.7 broadcast_in_dim.61
  181.8 408.8 %while.23 = (s32[]{:T(128)}, f32[2,72,32768]{2,0,1:T(2,128)}, bf16[2,4,128,4,64]{2,4,3,1,0:T(8,128)(2,1)}, s32[2,4,9]{2,1,0:T(4,128)S(1)}, bf16[2,4,128,4,64]{2,...) while((s32[]{:T(128)}, f32[2,72,32768]{2,0,1:T(2,128)}, ...), condition=%wide.region_12.15_spmd, body=%wide.region_7.14_spmd.sunk | while | flops 1868574720 | bytes 270851232 | solution.py:144
  182.2 8.2 gather_fusion.1
  195.1 8.0 reshape.262
  203.1 7.5 copy.197
  214.6 7.8 fusion.195
  222.4 7.3 fusion.193
  229.7 23.7 %fusion.197 = bf16[2,4,128,4,64]{2,4,3,1,0:T(8,128)(2,1)} fusion(bf16[2,4,128,4,64]{2,4,3,1,0:T(8,128)(2,1)} %get-tuple-element.308, s32[]{:T(128)S(6)} %copy.213, bf16[4,1152,4,64]{1,3,2,0:T(8,128)(2,1)S(1)} %copy-done.1, f32[4,4,128,1152]{3,2,1,0:T(8,128)} %fusion.195, f32[4,4,128,1152]{3,2,1,0:T(8,128)} %get-tuple-element.279, ...), kind=kOutput, calls=%fused_computation.52.clone.1 | convolution fusion | flops 318508160 | bytes 40648708 | tf_op jit(solution)/shard_map/while/body/eval_jaxpr/bhij,bjhe->bihe/dot_general | solution.py:127
  253.4 25.1 %fusion.196 = f32[4,1152,4,64]{1,3,2,0:T(8,128)} fusion(f32[4,4,128,1152]{3,2,1,0:T(8,128)} %fusion.195, bf16[2,4,128,4,64]{2,4,3,1,0:T(8,128)(2,1)} %get-tuple-element.318, s32[]{:T(128)S(6)} %copy.213, f32[4,4,128,1152]{3,2,1,0:T(8,128)} %get-tuple-element.279, f32[4,4,128]{2,1,0:T(4,128)S(1)} %get-tuple-element.277), kind=kOutput, calls=%fused_computation.50.clone.1 | convolution fusion | flops 318508160 | bytes 42745860 | tf_op jit(solution)/shard_map/while/body/eval_jaxpr/bhij,bihe->bjhe/dot_general | solution.py:130
  278.5 6.3 fusion.194
  284.8 9.5 %copy.198 = f32[4,1152,4,64]{3,2,1,0:T(4,128)} copy(f32[4,1152,4,64]{1,3,2,0:T(8,128)} %fusion.194) | data formatting | bytes 9437184 | tf_op jit(solution)/shard_map/while/body/eval_jaxpr/bhij,bihe->bjhe/transpose | solution.py:133
  294.3 10.3 %reshape.263 = f32[1,36,32768]{2,1,0:T(8,128)} reshape(f32[4,1152,4,64]{3,2,1,0:T(4,128)} %copy.198) | data formatting | bytes 9437184 | tf_op jit(solution)/shard_map/while/body/eval_jaxpr/stack;while/body/eval_jaxpr/reshape | solution.py:138
  304.6 9.5 %copy.199 = f32[4,1152,4,64]{3,2,1,0:T(4,128)} copy(f32[4,1152,4,64]{1,3,2,0:T(8,128)} %fusion.196) | data formatting | bytes 9437184 | tf_op jit(solution)/shard_map/while/body/eval_jaxpr/bhij,bihe->bjhe/transpose | solution.py:130
  314.2 10.3 %reshape.265 = f32[1,36,32768]{2,1,0:T(8,128)} reshape(f32[4,1152,4,64]{3,2,1,0:T(4,128)} %copy.199) | data formatting | bytes 9437184 | tf_op jit(solution)/shard_map/while/body/eval_jaxpr/stack;while/body/eval_jaxpr/reshape | solution.py:138
  324.5 4.8 maximum_bitcast_fusion.2
  329.3 7.9 copy.200
  337.2 48.8 %scatter_fusion = f32[2,72,32768]{2,0,1:T(2,128)} fusion(f32[2,72,32768]{2,0,1:T(2,128)} %get-tuple-element.307, s32[36]{0:T(128)S(1)} %fusion.191, f32[36,2,32768]{2,1,0:T(2,128)} %copy.200), kind=kCustom, calls=%fused_computation.3.clone.1 | custom fusion | flops 2359296 | bytes 28311696 | tf_op jit(solution)/shard_map/while/body/eval_jaxpr/scatter-add | solution.py:141
  386.3 8.2 gather_fusion.1
  399.2 8.0 reshape.262
  407.2 7.5 copy.197
  414.7 4.1 reshape.264
  418.8 7.8 fusion.195
  426.5 7.3 fusion.193
  433.8 23.7 %fusion.197 = bf16[2,4,128,4,64]{2,4,3,1,0:T(8,128)(2,1)} fusion(bf16[2,4,128,4,64]{2,4,3,1,0:T(8,128)(2,1)} %get-tuple-element.308, s32[]{:T(128)S(6)} %copy.213, bf16[4,1152,4,64]{1,3,2,0:T(8,128)(2,1)S(1)} %copy-done.1, f32[4,4,128,1152]{3,2,1,0:T(8,128)} %fusion.195, f32[4,4,128,1152]{3,2,1,0:T(8,128)} %get-tuple-element.279, ...), kind=kOutput, calls=%fused_computation.52.clone.1 | convolution fusion | flops 318508160 | bytes 40648708 | tf_op jit(solution)/shard_map/while/body/eval_jaxpr/bhij,bjhe->bihe/dot_general | solution.py:127
  457.6 25.1 %fusion.196 = f32[4,1152,4,64]{1,3,2,0:T(8,128)} fusion(f32[4,4,128,1152]{3,2,1,0:T(8,128)} %fusion.195, bf16[2,4,128,4,64]{2,4,3,1,0:T(8,128)(2,1)} %get-tuple-element.318, s32[]{:T(128)S(6)} %copy.213, f32[4,4,128,1152]{3,2,1,0:T(8,128)} %get-tuple-element.279, f32[4,4,128]{2,1,0:T(4,128)S(1)} %get-tuple-element.277), kind=kOutput, calls=%fused_computation.50.clone.1 | convolution fusion | flops 318508160 | bytes 42745860 | tf_op jit(solution)/shard_map/while/body/eval_jaxpr/bhij,bihe->bjhe/dot_general | solution.py:130
  482.7 6.3 fusion.194
  488.9 9.5 %copy.198 = f32[4,1152,4,64]{3,2,1,0:T(4,128)} copy(f32[4,1152,4,64]{1,3,2,0:T(8,128)} %fusion.194) | data formatting | bytes 9437184 | tf_op jit(solution)/shard_map/while/body/eval_jaxpr/bhij,bihe->bjhe/transpose | solution.py:133
  498.5 10.3 %reshape.263 = f32[1,36,32768]{2,1,0:T(8,128)} reshape(f32[4,1152,4,64]{3,2,1,0:T(4,128)} %copy.198) | data formatting | bytes 9437184 | tf_op jit(solution)/shard_map/while/body/eval_jaxpr/stack;while/body/eval_jaxpr/reshape | solution.py:138
  508.8 9.5 %copy.199 = f32[4,1152,4,64]{3,2,1,0:T(4,128)} copy(f32[4,1152,4,64]{1,3,2,0:T(8,128)} %fusion.196) | data formatting | bytes 9437184 | tf_op jit(solution)/shard_map/while/body/eval_jaxpr/bhij,bihe->bjhe/transpose | solution.py:130
  518.3 10.3 %reshape.265 = f32[1,36,32768]{2,1,0:T(8,128)} reshape(f32[4,1152,4,64]{3,2,1,0:T(4,128)} %copy.199) | data formatting | bytes 9437184 | tf_op jit(solution)/shard_map/while/body/eval_jaxpr/stack;while/body/eval_jaxpr/reshape | solution.py:138
  528.6 4.8 maximum_bitcast_fusion.2
  533.4 7.9 copy.200
  541.3 48.9 %scatter_fusion = f32[2,72,32768]{2,0,1:T(2,128)} fusion(f32[2,72,32768]{2,0,1:T(2,128)} %get-tuple-element.307, s32[36]{0:T(128)S(1)} %fusion.191, f32[36,2,32768]{2,1,0:T(2,128)} %copy.200), kind=kCustom, calls=%fused_computation.3.clone.1 | custom fusion | flops 2359296 | bytes 28311696 | tf_op jit(solution)/shard_map/while/body/eval_jaxpr/scatter-add | solution.py:141
  590.6 9.4 %slice.60 = bf16[2,64,32768]{2,0,1:T(2,128)(2,1)} slice(f32[2,72,32768]{2,0,1:T(2,128)} %get-tuple-element.73), slice={[0:2], [8:72], [0:32768]} | slice | bytes 16777216 | tf_op jit(solution)/shard_map/slice | solution.py:149
  600.0 14.0 %reshape.225 = bf16[2,32,2,128,256]{4,3,0,2,1:T(8,128)(2,1)} reshape(bf16[2,64,32768]{2,0,1:T(2,128)(2,1)} %slice.60) | data formatting | bytes 16777216 | tf_op jit(solution)/shard_map/reshape | solution.py:151
  614.0 7.8 copy.137
  621.8 11.2 %all-to-all-start.2 = ((bf16[2,32,2,128,256]{4,3,2,0,1:T(8,128)(2,1)}), bf16[2,32,2,128,256]{4,3,2,0,1:T(8,128)(2,1)}, u32[]{:S(2)}, u32[]{:S(2)}) async-start(bf16[2,32,2,128,256]{4,3,2,0,1:T(8,128)(2,1)} %copy.137), calls=%async_computation.3 | async-start | bytes 16777216 | tf_op jit(solution)/shard_map/all_to_all | solution.py:153
  633.0 85.3 %while.22 = (s32[]{:T(128)}, bf16[2,4,128,4,64]{2,1,0,4,3:T(4,128)(2,1)}, s32[2,4,9]{2,1,0:T(4,128)S(1)}, bf16[2,72,128,256]{3,2,1,0:T(8,128)(2,1)}, bf16[2,4,128,4,64]{2,4,3,1,0:T(8,128)(2,1)S(1)}, /*index=5*/s32[]{:T(128)}) while((s32[]{:T(128)}, bf16[2,4,128,4,64]{2,1,0,4,3:T(4,128)(2,1)}, s32[2,4,9]{2,1,0:T(4,128)S(1)}, ...), condition=%wide.region_5.8_spmd, body=%wide.region_2.7_spmd.sunk | while | flops 618269120 | bytes 66606568 | solution.py:96
  633.2 8.2 gather_fusion
  646.1 8.0 reshape.254
  658.1 9.3 %fusion.176 = (f32[4,4,128]{2,1,0:T(4,128)S(1)}, f32[4,4,128,1152]{3,2,1,0:T(8,128)}) fusion(bf16[4,1152,4,64]{3,2,1,0:T(4,128)(2,1)} %reshape.254, bf16[2,4,128,4,64]{2,4,3,1,0:T(8,128)(2,1)S(1)} %get-tuple-element.296, s32[]{:T(128)S(6)} %copy.206), kind=kOutput, calls=%fused_computation.129.clone.1 | convolution fusion | flops 309068928 | bytes 12066820 | tf_op jit(solution)/shard_map/while/body/eval_jaxpr/sub | solution.py:34
  667.4 7.2 fusion.177
  675.8 8.2 gather_fusion
  688.7 8.0 reshape.254
  700.8 9.3 %fusion.176 = (f32[4,4,128]{2,1,0:T(4,128)S(1)}, f32[4,4,128,1152]{3,2,1,0:T(8,128)}) fusion(bf16[4,1152,4,64]{3,2,1,0:T(4,128)(2,1)} %reshape.254, bf16[2,4,128,4,64]{2,4,3,1,0:T(8,128)(2,1)S(1)} %get-tuple-element.296, s32[]{:T(128)S(6)} %copy.206), kind=kOutput, calls=%fused_computation.129.clone.1 | convolution fusion | flops 309068928 | bytes 12066820 | tf_op jit(solution)/shard_map/while/body/eval_jaxpr/sub | solution.py:34
  710.1 7.2 fusion.177
  721.9 18.2 %copy.135 = f32[2,72,32768]{2,1,0:T(8,128)} copy(f32[2,72,32768]{2,0,1:T(2,128)} %get-tuple-element.73) | data formatting | bytes 37748736 | tf_op jit(solution)/shard_map/while | solution.py:144
  743.4 7.8 copy.138
  751.2 13.5 %reshape.172 = bf16[2,64,32768]{2,1,0:T(8,128)(2,1)} reshape(bf16[2,32,2,128,256]{4,3,2,1,0:T(8,128)(2,1)} %copy.138) | data formatting | bytes 16777216 | tf_op jit(solution)/shard_map/reshape | solution.py:160
  764.7 6.3 fusion.100
  775.7 4.6 fusion.106
  786.0 5.0 bitcast_convert_fusion
  795.5 69.1 %reduce-scatter.8.cloned.1.call-done = bf16[32,1024]{1,0:T(8,128)(2,1)} async-done(((bf16[1024,1024]{1,0:T(8,128)(2,1)}), bf16[32,1024]{1,0:T(8,128)(2,1)}) %reduce-scatter.8.cloned.1.call-update) | async-done | bytes 65552 | tf_op jit(solution)/shard_map/reduce_scatter | solution.py:173
  867.5 30.1 %reduce-scatter.6.cloned.1.call-done = bf16[1024,256]{1,0:T(8,128)(2,1)} async-done(((bf16[1024,1024]{1,0:T(8,128)(2,1)}), bf16[1024,256]{1,0:T(8,128)(2,1)}) %reduce-scatter.6.cloned.1.call-update) | async-done | bytes 524304 | tf_op jit(solution)/shard_map/reduce_scatter | solution.py:191
  899.4 6.7 all-reduce
  (134 shorter events, 82.5 us)
Async XLA Ops:
  7.2 89.8 %copy-start = (bf16[256,1024]{1,0:T(8,128)(2,1)S(1)}, bf16[256,1024]{1,0:T(8,128)(2,1)}, u32[]{:S(2)}) copy-start(bf16[256,1024]{1,0:T(8,128)(2,1)} %param.16) | copy-start | bytes 1572868
  7.2 17.8 %copy-start.2 = (bf16[1024,1024]{1,0:T(8,128)(2,1)S(1)}, bf16[1024,1024]{1,0:T(8,128)(2,1)}, u32[]{:S(2)}) copy-start(bf16[1024,1024]{1,0:T(8,128)(2,1)} %param.14) | copy-start | bytes 6291460
  8.7 21.4 %all-to-all-start = ((s32[32,1,2]{2,1,0:T(1,128)}), s32[32,1,2]{2,1,0:T(1,128)S(1)}, u32[]{:S(2)}, u32[]{:S(2)}) async-start(s32[32,1,2]{2,1,0:T(1,128)} %copy.125), calls=%async_computation | async-start | bytes 32768 | tf_op jit(solution)/shard_map/all_to_all | solution.py:74
  20.1 8.3 copy-start.13
  22.4 6.0 copy-start.11
  28.4 1.2 copy-start.4
  31.4 5.4 copy-start.15
  52.1 8.3 slice-start
  52.1 107.3 %all-to-all-start.1 = ((bf16[2,32,2,128,256]{4,3,2,0,1:T(8,128)(2,1)}), bf16[2,32,2,128,256]{4,3,2,0,1:T(8,128)(2,1)}, u32[]{:S(2)}, u32[]{:S(2)}) async-start(bf16[2,32,2,128,256]{4,3,2,0,1:T(8,128)(2,1)} %copy.127), calls=%async_computation.1 | async-start | bytes 16777216 | tf_op jit(solution)/shard_map/all_to_all | solution.py:79
  59.7 37.3 %all-gather.2.cloned.1.call-start = ((), (), s32[]{:S(2)}) async-start(), calls=%async_computation.7 | async-start | bytes 2621440 | tf_op jit(solution)/shard_map/all_gather | solution.py:103
  175.0 6.7 copy-start.10
  214.6 7.8 copy-start.1
  418.8 7.8 copy-start.1
  621.8 11.2 %copy-start.7 = (bf16[2,4,128,4,64]{2,4,3,1,0:T(8,128)(2,1)S(1)}, bf16[2,4,128,4,64]{2,4,3,1,0:T(8,128)(2,1)}, u32[]{:S(2)}) copy-start(bf16[2,4,128,4,64]{2,4,3,1,0:T(8,128)(2,1)} %get-tuple-element.340) | copy-start | bytes 1572868
  621.8 121.6 %all-to-all-start.2 = ((bf16[2,32,2,128,256]{4,3,2,0,1:T(8,128)(2,1)}), bf16[2,32,2,128,256]{4,3,2,0,1:T(8,128)(2,1)}, u32[]{:S(2)}, u32[]{:S(2)}) async-start(bf16[2,32,2,128,256]{4,3,2,0,1:T(8,128)(2,1)} %copy.137), calls=%async_computation.3 | async-start | bytes 16777216 | tf_op jit(solution)/shard_map/all_to_all | solution.py:153
  633.0 160.5 %reduce-scatter.4.cloned.1.call-start = ((), (), s32[]{:S(2)}) async-start(), calls=%async_computation.6 | async-start | bytes 2621440 | tf_op jit(solution)/shard_map/reduce_scatter | solution.py:98
  667.4 7.2 copy-start.8
  674.9 0.8 copy-start.9
  710.1 7.2 copy-start.8
  717.6 0.8 copy-start.9
  721.9 142.7 %reduce-scatter.8.cloned.1.call-start = ((), (), s32[]{:S(2)}) async-start(), calls=%async_computation.9 | async-start | bytes 2162688 | tf_op jit(solution)/shard_map/reduce_scatter | solution.py:173
  721.9 18.2 %copy-start.17 = (bf16[1024,1024]{1,0:T(8,128)(2,1)S(1)}, bf16[1024,1024]{1,0:T(8,128)(2,1)}, u32[]{:S(2)}) copy-start(bf16[1024,1024]{1,0:T(8,128)(2,1)} %all-gather.2.cloned.1.call-done) | copy-start | bytes 6291460
  740.1 1.1 copy-start.6
  751.2 13.5 %copy-start.16 = (s32[64]{0:T(128)S(1)}, s32[64]{0:T(128)}, u32[]{:S(2)}) copy-start(s32[64]{0:T(128)} %copy-done.15) | copy-start | bytes 772
  764.7 10.9 %copy-start.3 = (bf16[1024,1024]{1,0:T(8,128)(2,1)S(1)}, bf16[1024,1024]{1,0:T(8,128)(2,1)}, u32[]{:S(2)}) copy-start(bf16[1024,1024]{1,0:T(8,128)(2,1)} %param.14) | copy-start | bytes 6291460
  764.7 10.9 %copy-start.12 = (f32[1024]{0:T(1024)S(1)}, f32[1024]{0:T(1024)}, u32[]{:S(2)}) copy-start(f32[1024]{0:T(1024)} %copy-done.11) | copy-start | bytes 12292
  764.7 10.9 %copy-start.14 = (f32[1024]{0:T(1024)S(1)}, f32[1024]{0:T(1024)}, u32[]{:S(2)}) copy-start(f32[1024]{0:T(1024)} %copy-done.13) | copy-start | bytes 12292
  785.9 111.7 %reduce-scatter.6.cloned.1.call-start = ((), (), s32[]{:S(2)}) async-start(), calls=%async_computation.8 | async-start | bytes 2621440 | tf_op jit(solution)/shard_map/reduce_scatter | solution.py:191
  791.0 115.0 %copy-start.5 = (bf16[1024,256]{1,0:T(8,128)(2,1)S(1)}, bf16[1024,256]{1,0:T(8,128)(2,1)}, u32[]{:S(2)}) copy-start(bf16[1024,256]{1,0:T(8,128)(2,1)} %param.19) | copy-start | bytes 1572868
Sparse Core Ops, SparseCore 0:
  62.2 34.7 all-gather.1
  722.0 31.0 reduce-scatter.3
  786.0 78.5 reduce-scatter.7
  867.0 30.6 reduce-scatter.5
where the time goes:
time: 930 us; the launch traced here: 915 us
  local copies, waits for them, and re-layouts  322 us (35%)
  matrix products  198 us (21%)
  waiting for transfers between devices  194 us (21%)
  other arithmetic  152 us (16%)
  starting transfers between devices  28.3 us (3%)
  between operations  14.3 us (2%)
    scatter-add x2, other arithmetic, backward_block(): return (totals.at[:, flat_entries].add(both_grads), grad_query)  97.7 us
    reduce_scatter x1, waiting for transfers between devices, on_device(): lax.psum_scatter(jnp.concatenate([input_part.reshape(model_width // peer_...  69.1 us
    all_to_all x1, waiting for transfers between devices, on_device(): lax.all_to_all(outgoing, 'space', split_axis=1, concat_axis=1, tiled=True)  59.1 us
    dot_general x2, matrix products, backward_block(): jnp.einsum('bhij,bihe->bjhe', grad_score, block_queries, preferred_elemen...  50.2 us
    dot_general x2, matrix products, backward_block(): jnp.einsum('bhij,bjhe->bihe', grad_score, key_part, preferred_element_typ...  47.5 us
    reshape x4, local copies, waits for them, and re-layouts, backward_block(): jnp.stack([grad_key.reshape(entry_count, -1), grad_value.reshape(entry_co...  41.3 us
    all_gather x1, waiting for transfers between devices, on_device(): cotangent_full = lax.all_gather(cotangent, 'head', axis=1, tiled=True)  35.3 us
    sub x4, matrix products, probabilities(): weights = jnp.exp(scores - row_top)  33.2 us
  transfers between devices with their start and end apart: 7, of which 4 were waited for; matrix products, arithmetic and copies ran while one was open for 20% of the time, Pallas kernels for 0%

commit v1 on v0

v1 whole, which is shorter than its diff:
```python
import functools

import jax
import jax.numpy as jnp
from jax import lax
from jax.experimental import pallas as pl
from jax.experimental.pallas import tpu as pltpu
from jax.sharding import PartitionSpec as P

HEAD_DIM = 64
NEIGHBOURS = 9
NEAR = 4
EPSILON = 1e-05
F32 = jnp.float32
BF16 = jnp.bfloat16
VMEM_BYTES = 60 * 2**20


def dot(a, b, dims):
    return lax.dot_general(a, b, (dims, ((), ())), preferred_element_type=F32)


def norm_rows(tokens):
    values = tokens.astype(F32)
    mean = jnp.mean(values, axis=1, keepdims=True)
    centred = values - mean
    inverse = lax.rsqrt(jnp.mean(centred * centred, axis=1, keepdims=True) + EPSILON)
    return centred * inverse, mean, inverse


def head_cut(h):
    return slice(h * HEAD_DIM, (h + 1) * HEAD_DIM)


def project_kernel(heads, tokens_ref, w_ref, normed_ref, q_ref, kv_ref, mean_ref, inverse_ref):
    standard, mean, inverse = norm_rows(tokens_ref[...])
    normed = standard.astype(BF16)
    normed_ref[...] = normed
    mean_ref[...] = mean
    inverse_ref[...] = inverse
    q = dot(normed, w_ref[0], ((1,), (0,))).astype(BF16)
    q_ref[...] = (q.astype(F32) * HEAD_DIM ** (-0.5)).astype(BF16)
    k = dot(normed, w_ref[1], ((1,), (0,))).astype(BF16)
    v = dot(normed, w_ref[2], ((1,), (0,))).astype(BF16)
    for h in range(heads):
        pair = jnp.concatenate([k[:, head_cut(h)], v[:, head_cut(h)]], 1)
        kv_ref[:, h] = pair.reshape(kv_ref.shape[0], kv_ref.shape[2], 2 * HEAD_DIM)


def project(tokens, w3, tile_rows):
    rows, width = tokens.shape
    cols = w3.shape[2]
    step = 256
    kv_block = (step // tile_rows, cols // HEAD_DIM, tile_rows, 2 * HEAD_DIM)
    return pl.pallas_call(
        functools.partial(project_kernel, cols // HEAD_DIM),
        grid=(rows // step,),
        in_specs=[
            pl.BlockSpec((step, width), lambda i: (i, 0)),
            pl.BlockSpec((3, width, cols), lambda i: (0, 0, 0)),
        ],
        out_specs=[
            pl.BlockSpec((step, width), lambda i: (i, 0)),
            pl.BlockSpec((step, cols), lambda i: (i, 0)),
            pl.BlockSpec(kv_block, lambda i: (i, 0, 0, 0)),
            pl.BlockSpec((step, 1), lambda i: (i, 0)),
            pl.BlockSpec((step, 1), lambda i: (i, 0)),
        ],
        out_shape=[
            jax.ShapeDtypeStruct((rows, width), BF16),
            jax.ShapeDtypeStruct((rows, cols), BF16),
            jax.ShapeDtypeStruct((rows // tile_rows,) + kv_block[1:], BF16),
            jax.ShapeDtypeStruct((rows, 1), F32),
            jax.ShapeDtypeStruct((rows, 1), F32),
        ],
        compiler_params=pltpu.CompilerParams(vmem_limit_bytes=VMEM_BYTES),
    )(tokens, w3)


def pick_kernel(wanted_ref, kv_ref, out_ref):
    first = pl.program_id(0) * out_ref.shape[0]
    for i in range(out_ref.shape[0]):
        out_ref[i] = kv_ref[jnp.maximum(wanted_ref[first + i], 0)]


def pick_tiles(wanted, kv):
    count = wanted.shape[0]
    step = 8
    return pl.pallas_call(
        pick_kernel,
        grid_spec=pltpu.PrefetchScalarGridSpec(
            num_scalar_prefetch=1,
            grid=(count // step,),
            in_specs=[pl.BlockSpec(kv.shape, lambda i, wanted: (0, 0, 0, 0))],
            out_specs=pl.BlockSpec((step,) + kv.shape[1:], lambda i, wanted: (i, 0, 0, 0)),
        ),
        out_shape=jax.ShapeDtypeStruct((count,) + kv.shape[1:], kv.dtype),
        compiler_params=pltpu.CompilerParams(vmem_limit_bytes=VMEM_BYTES),
    )(wanted, kv)


def attention_kernel(entries_ref, q_ref, cot_ref, w_out_ref, normed_ref, *refs):
    kv_refs = refs[:NEIGHBOURS]
    att_out_ref, near_ref, far_ref, dq_ref, grad_out_ref, grad_q_ref = refs[NEIGHBOURS:-2]
    far_total, held = refs[-2:]
    tile = pl.program_id(0)
    last = pl.num_programs(0) - 1
    heads = q_ref.shape[1] // HEAD_DIM
    own = near_ref.shape[0]

    @pl.when(tile == 0)
    def _():
        near_ref[...] = jnp.zeros_like(near_ref)
        grad_out_ref[...] = jnp.zeros_like(grad_out_ref)
        grad_q_ref[...] = jnp.zeros_like(grad_q_ref)

        @pl.loop(0, far_total.shape[0])
        def _(i):
            far_total[i] = jnp.zeros(far_total.shape[1:], F32)

    cot = cot_ref[...]
    grad_attended = dot(cot, w_out_ref[...], ((1,), (1,))).astype(BF16)
    q = q_ref[...]
    left = lax.broadcasted_iota(jnp.int32, (128, 128), 1) < HEAD_DIM
    mixed_t = []
    for h in range(heads):
        cut = head_cut(h)
        pair = jnp.concatenate([q[:, cut], grad_attended[:, cut]], 1)
        zero = jnp.zeros_like(pair)
        stacked = jnp.concatenate([jnp.where(left, pair, zero), jnp.where(left, zero, pair)], 0)
        kv = jnp.concatenate([r[0, h] for r in kv_refs], 0)
        both = dot(kv, stacked, ((1,), (1,)))
        scores = both[:, :128]
        grad_prob = both[:, 128:]
        weights = jnp.exp(scores - jnp.max(scores, axis=0, keepdims=True))
        inverse = 1.0 / jnp.sum(weights, axis=0, keepdims=True)
        row_delta = jnp.sum(weights * grad_prob, axis=0, keepdims=True) * inverse
        likely = weights * inverse
        grad_score = likely * (grad_prob - row_delta)
        factors = jnp.concatenate([grad_score.astype(BF16), likely.astype(BF16)], 1)
        grad_kv = dot(factors, stacked, ((1,), (0,)))
        for j in range(NEIGHBOURS):
            held[j, h] = grad_kv[j * 128 : (j + 1) * 128]
        mixed_t.append(dot(kv, factors, ((0,), (0,))))

    @pl.loop(0, NEAR)
    def _(j):
        near_ref[entries_ref[tile, j]] += held[j]

    @pl.loop(NEAR, NEIGHBOURS)
    def _(j):
        far_total[entries_ref[tile, j] - own] += held[j]

    dq_t = jnp.concatenate([m[:HEAD_DIM, :128] for m in mixed_t], 0)
    att_t = jnp.concatenate([m[HEAD_DIM:, 128:] for m in mixed_t], 0)
    dq = (dq_t.T * HEAD_DIM ** (-0.5)).astype(BF16)
    attended = att_t.T.astype(BF16)
    dq_ref[...] = dq
    att_out_ref[...] = dot(attended, w_out_ref[...], ((1,), (0,))).astype(BF16)
    grad_out_ref[...] += dot(cot, attended, ((0,), (0,)))
    grad_q_ref[...] += dot(normed_ref[...], dq, ((0,), (0,)))

    @pl.when(tile == last)
    def _():
        @pl.loop(0, far_total.shape[0])
        def _(i):
            far_ref[i] = far_total[i].astype(BF16)


def attention(entries, q, cot, w_out, normed, kv, fetched):
    tiles, heads, rows, mixed = kv.shape
    slots = fetched.shape[0]
    tile_block = (1, heads, rows, mixed)
    cols = q.shape[1]
    width = cot.shape[1]
    whole2 = lambda t, e: (0, 0)
    row2 = lambda t, e: (t, 0)
    kv_specs = []
    for j in range(NEIGHBOURS):
        if j < NEAR:
            kv_specs.append(pl.BlockSpec(tile_block, lambda t, e, j=j: (e[t, j], 0, 0, 0)))
        else:
            kv_specs.append(
                pl.BlockSpec(tile_block, lambda t, e, j=j: (e[t, j] - tiles, 0, 0, 0))
            )
    once = pl.Buffered(1)
    return pl.pallas_call(
        attention_kernel,
        grid_spec=pltpu.PrefetchScalarGridSpec(
            num_scalar_prefetch=1,
            grid=(tiles,),
            in_specs=[
                pl.BlockSpec((rows, cols), row2),
                pl.BlockSpec((rows, width), row2),
                pl.BlockSpec((cols, width), whole2),
                pl.BlockSpec((rows, width), row2),
            ]
            + kv_specs,
            out_specs=[
                pl.BlockSpec((rows, width), row2),
                pl.BlockSpec(kv.shape, lambda t, e: (0, 0, 0, 0), pipeline_mode=once),
                pl.BlockSpec(fetched.shape, lambda t, e: (0, 0, 0, 0), pipeline_mode=once),
                pl.BlockSpec((rows, cols), row2),
                pl.BlockSpec((width, cols), whole2, pipeline_mode=once),
                pl.BlockSpec((width, cols), whole2, pipeline_mode=once),
            ],
            scratch_shapes=[
                pltpu.VMEM(fetched.shape, F32),
                pltpu.VMEM((NEIGHBOURS,) + kv.shape[1:], F32),
            ],
        ),
        out_shape=[
            jax.ShapeDtypeStruct((tiles * rows, width), BF16),
            jax.ShapeDtypeStruct(kv.shape, F32),
            jax.ShapeDtypeStruct(fetched.shape, BF16),
            jax.ShapeDtypeStruct((tiles * rows, cols), BF16),
            jax.ShapeDtypeStruct((width, cols), F32),
            jax.ShapeDtypeStruct((width, cols), F32),
        ],
        compiler_params=pltpu.CompilerParams(vmem_limit_bytes=VMEM_BYTES),
    )(entries, q, cot, w_out, normed, *([kv] * NEAR + [fetched] * (NEIGHBOURS - NEAR)))


def place_kernel(wanted_ref, near_ref, back_ref, grad_kv_ref, total):
    step = pl.program_id(0)
    count = back_ref.shape[0]

    @pl.when(step == 0)
    def _():
        total[...] = near_ref[...]

    for i in range(count):
        tile = wanted_ref[step * count + i]

        @pl.when(tile >= 0)
        def _():
            total[tile] += back_ref[i].astype(F32)

    @pl.when(step == pl.num_programs(0) - 1)
    def _():
        grad_kv_ref[...] = total[...].astype(BF16)


def place(wanted, near, back):
    slots = back.shape[0]
    step = 8
    whole = lambda i, w: (0, 0, 0, 0)
    return pl.pallas_call(
        place_kernel,
        grid_spec=pltpu.PrefetchScalarGridSpec(
            num_scalar_prefetch=1,
            grid=(slots // step,),
            in_specs=[
                pl.BlockSpec(near.shape, whole),
                pl.BlockSpec((step,) + back.shape[1:], lambda i, w: (i, 0, 0, 0)),
            ],
            out_specs=pl.BlockSpec(near.shape, whole),
            scratch_shapes=[pltpu.VMEM(near.shape, F32)],
        ),
        out_shape=jax.ShapeDtypeStruct(near.shape, BF16),
        compiler_params=pltpu.CompilerParams(vmem_limit_bytes=VMEM_BYTES),
    )(wanted, near, back)


def finish_kernel(heads, tokens_ref, dq_ref, grad_kv_ref, w_ref, part_ref, sums_ref, grad_w_ref, total):
    step = pl.program_id(0)

    @pl.when(step == 0)
    def _():
        total[...] = jnp.zeros_like(total)

    standard, _, _ = norm_rows(tokens_ref[...])
    pairs = [grad_kv_ref[:, h].reshape(standard.shape[0], 2 * HEAD_DIM) for h in range(heads)]
    dk = jnp.concatenate([p[:, :HEAD_DIM] for p in pairs], 1)
    dv = jnp.concatenate([p[:, HEAD_DIM:] for p in pairs], 1)
    total[...] += dot(standard.astype(BF16), jnp.concatenate([dk, dv], 1), ((0,), (0,)))
    part = dot(dq_ref[...], w_ref[0], ((1,), (1,)))
    part += dot(dk, w_ref[1], ((1,), (1,)))
    part += dot(dv, w_ref[2], ((1,), (1,)))
    sums = [jnp.sum(part, 1, keepdims=True), jnp.sum(part * standard, 1, keepdims=True)]
    sums_ref[...] = jnp.concatenate(sums, 1)
    part_ref[...] = part.astype(BF16)

    @pl.when(step == pl.num_programs(0) - 1)
    def _():
        grad_w_ref[...] = total[...].astype(BF16)


def finish(tokens, dq, grad_kv, w3):
    rows, width = tokens.shape
    cols = dq.shape[1]
    step = 256
    row2 = lambda i: (i, 0)
    return pl.pallas_call(
        functools.partial(finish_kernel, cols // HEAD_DIM),
        grid=(rows // step,),
        in_specs=[
            pl.BlockSpec((step, width), row2),
            pl.BlockSpec((step, cols), row2),
            pl.BlockSpec((step // grad_kv.shape[2],) + grad_kv.shape[1:], lambda i: (i, 0, 0, 0)),
            pl.BlockSpec((3, width, cols), lambda i: (0, 0, 0)),
        ],
        out_specs=[
            pl.BlockSpec((step, width), row2),
            pl.BlockSpec((step, 2), row2),
            pl.BlockSpec((width, 2 * cols), lambda i: (0, 0)),
        ],
        out_shape=[
            jax.ShapeDtypeStruct((rows, width), BF16),
            jax.ShapeDtypeStruct((rows, 2), F32),
            jax.ShapeDtypeStruct((width, 2 * cols), BF16),
        ],
        scratch_shapes=[pltpu.VMEM((width, 2 * cols), F32)],
        compiler_params=pltpu.CompilerParams(vmem_limit_bytes=VMEM_BYTES),
    )(tokens, dq, grad_kv, w3)


def exchange(array):
    return lax.all_to_all(array, "space", split_axis=0, concat_axis=0, tiled=True)


def sum_rows(part, peers):
    width, cols = part.shape
    arrived = exchange(part.reshape(peers, width // peers, cols))
    return jnp.sum(arrived.astype(F32), 0)


def on_device(tokens, w_qkv, w_out, neighbours, requests, cotangent):
    row_count, width = tokens.shape
    tiles = neighbours.shape[0]
    rows = row_count // tiles
    cols = w_qkv.shape[2]
    peers = lax.axis_size("space")
    slot_count = requests.shape[2]
    share = cotangent.shape[1]
    column = lax.axis_index("head") * share
    w3 = jnp.transpose(w_qkv, (1, 0, 2))

    incoming = exchange(requests.reshape(peers, slot_count)).reshape(-1)
    cot_full = lax.all_gather(cotangent, "head", axis=1, tiled=True)
    normed, q, kv, mean, inverse = project(tokens, w3, rows)
    outgoing = pick_tiles(incoming, kv)
    fetched = exchange(outgoing.reshape((peers, slot_count) + kv.shape[1:]))
    fetched = fetched.reshape(outgoing.shape)
    att_out, near, far, dq, grad_out, grad_q = attention(
        neighbours, q, cot_full, w_out, normed, kv, fetched
    )
    back = exchange(far.reshape((peers, slot_count) + kv.shape[1:]))
    summed = lax.psum_scatter(att_out, "head", scatter_dimension=1, tiled=True)
    early = sum_rows(jnp.concatenate([grad_out, grad_q], 1).astype(BF16), peers)
    grad_kv = place(incoming, near, back.reshape(outgoing.shape))
    part, sums, grad_w_kv = finish(tokens, dq, grad_kv, w3)
    late = sum_rows(grad_w_kv, peers)
    own_part = lax.psum_scatter(part, "head", scatter_dimension=1, tiled=True).astype(F32)
    sums = lax.psum(sums, "head") / width

    own_tokens = lax.dynamic_slice_in_dim(tokens, column, share, 1).astype(F32)
    layer_out = (own_tokens + summed.astype(F32)).astype(BF16)
    own_standard = (own_tokens - mean) * inverse
    grad_tokens = (
        cotangent.astype(F32) + inverse * (own_part - sums[:, :1] - own_standard * sums[:, 1:])
    ).astype(BF16)
    grad_w_qkv = jnp.concatenate([early[:, cols:], late], 1).reshape(-1, 3, cols)
    grad_w_out = early[:, :cols].T
    return (layer_out, grad_tokens, grad_w_qkv, grad_w_out)


def solution(mesh):
    placed = (
        P("space", None),
        P(None, None, "head"),
        P("head", None),
        P("space", None),
        P("space", None, None),
        P("space", "head"),
    )
    return jax.shard_map(
        on_device,
        mesh=mesh,
        in_specs=placed,
        out_specs=(
            P("space", "head"),
            P("space", "head"),
            P("space", None, "head"),
            P("head", "space"),
        ),
        check_vma=False,
    )
```

time: 930 us -> 388 us (0.42); the launches traced: 915 us -> 384 us
  local copies, waits for them, and re-layouts: 322 us -> 5.76 us
  matrix products: 198 us -> 0 us
  other arithmetic: 152 us -> 4.34 us
  Pallas kernels: 0 us -> 83 us
  blocking collectives: 6.67 us -> 46 us
    dot_general x17 -> x0, matrix products: 165 us -> none  [the longest x2 50.2 us: backward_block(): jnp.einsum('bhij,bihe->bjhe', grad_score, block_queries, preferred_elemen...]
    all_to_all x3 -> x4, waiting for transfers between devices: 59.1 us -> 162 us  [exchange(): lax.all_to_all(array, 'space', split_axis=0, concat_axis=0, tiled=True)]
    reduce_scatter x3 -> x2, waiting for transfers between devices: 99.3 us -> 0.01 us  [the longest x1 0.01 us: on_device(): summed = lax.psum_scatter(att_out, 'head', scatter_dimension=1, tiled=True)]
    scatter-add x2 -> x0, other arithmetic: 97.7 us -> none  [backward_block(): return (totals.at[:, flat_entries].add(both_grads), grad_query)]
    reshape x23 -> x2, local copies, waits for them, and re-layouts: 94 us -> 1.26 us  [the longest x1 0.65 us: on_device(): jnp.concatenate([early[:, cols:], late], 1).reshape(-1, 3, cols)]
    pallas_call x0 -> x5, Pallas kernels: none -> 83 us  [the longest x1 53.1 us: attention(): pl.pallas_call(attention_kernel, grid_spec=pltpu.PrefetchScalarGridSpec(n...]
    squeeze x10 -> x0, local copies, waits for them, and re-layouts: 63.2 us -> none  [the longest x4 31 us: backward_block(): key_part = keyset[0]]
    transpose x6 -> x1, local copies, waits for them, and re-layouts: 39.3 us -> 0.62 us  [on_device(): grad_w_out = early[:, :cols].T]
  transfers between devices with their start and end apart: 7 -> 7, of which waited for: 4 -> 4; matrix products, arithmetic and copies ran while one was open for 20% -> 1% of each run, Pallas kernels for 0% -> 6%
where the time goes in v1:
time: 388 us; the launch traced here: 384 us
  waiting for transfers between devices  200 us (52%)
  Pallas kernels  83 us (21%)
  blocking collectives  46 us (12%)
  starting transfers between devices  31.4 us (8%)
  between operations  13.9 us (4%)
  local copies, waits for them, and re-layouts  5.76 us (1%)
  other arithmetic  4.34 us (1%)
    all_to_all x4, waiting for transfers between devices, exchange(): lax.all_to_all(array, 'space', split_axis=0, concat_axis=0, tiled=True)  162 us
    pallas_call x1, Pallas kernels, attention(): pl.pallas_call(attention_kernel, grid_spec=pltpu.PrefetchScalarGridSpec(n...  53.1 us
    all_gather x1, waiting for transfers between devices, on_device(): cot_full = lax.all_gather(cotangent, 'head', axis=1, tiled=True)  36.6 us
    all_to_all x4, starting transfers between devices, exchange(): lax.all_to_all(array, 'space', split_axis=0, concat_axis=0, tiled=True)  31.3 us
    all_to_all x1, blocking collectives, exchange(): lax.all_to_all(array, 'space', split_axis=0, concat_axis=0, tiled=True)  26.5 us
    psum x1, blocking collectives, on_device(): sums = lax.psum(sums, 'head') / width  19.4 us
    pallas_call x1, Pallas kernels, place(): pl.pallas_call(place_kernel, grid_spec=pltpu.PrefetchScalarGridSpec(num_s...  8.62 us
    pallas_call x1, Pallas kernels, finish(): pl.pallas_call(functools.partial(finish_kernel, cols // HEAD_DIM), grid=(...  8.49 us
  transfers between devices with their start and end apart: 7, of which 4 were waited for; matrix products, arithmetic and copies ran while one was open for 1% of the time, Pallas kernels for 6%

profile of v1, /device:TPU:1, one launch (start us, length us, event | category | flops | bytes accessed | tf_op | source)
XLA Modules:
  0.0 384.4 jit_solution(8945807214986710959)
XLA Ops:
  7.2 1.4 copy.13
  8.5 9.4 %all-to-all-start = ((s32[32,1,2]{2,1,0:T(1,128)}), s32[32,1,2]{2,1,0:T(1,128)S(1)}, u32[]{:S(2)}, u32[]{:S(2)}) async-start(s32[32,1,2]{2,1,0:T(1,128)} %copy.13), calls=%async_computation | async-start | bytes 32768 | tf_op jit(solution)/shard_map/all_to_all | solution.py:319
  18.0 6.3 %shard_map.93 = (bf16[1024,1024]{1,0:T(8,128)(2,1)}, bf16[1024,256]{1,0:T(8,128)(2,1)}, bf16[8,4,128,128]{3,2,1,0:T(8,128)(2,1)}, f32[1024,1]{1,0:T(8,128)}, f32[1024,1]{1,0:T(8,128)}) custom-call(bf16[1024,1024]{1,0:T(8,128)(2,1)} %tokens_ref.3, bf16[3,1024,256]{2,1,0:T(8,128)(2,1)} %bitcast.17), custom_call_target="tpu_custom_call" | custom-call | tf_op jit(solution)/shard_map/pallas_call | solution.py:55
  24.2 0.6 all-to-all-done
  24.8 0.5 broadcast.8
  25.3 0.7 reduce.9
  26.0 0.6 reshape.39.wanted_ref
  26.7 6.5 %shard_map.94 = bf16[64,4,128,128]{3,2,1,0:T(8,128)(2,1)} custom-call(s32[64]{0:T(128)} %reshape.39.wanted_ref, bf16[8,4,128,128]{3,2,1,0:T(8,128)(2,1)} %get-tuple-element.20.kv_ref.refs_0_.refs_1_.refs_2_.refs_3_), custom_call_target="tpu_custom_call" | custom-call | tf_op jit(solution)/shard_map/pallas_call | solution.py:89
  33.2 6.9 %all-to-all-start.1 = ((bf16[32,2,4,128,128]{4,3,2,1,0:T(8,128)(2,1)}), bf16[32,2,4,128,128]{4,3,2,1,0:T(8,128)(2,1)}, u32[]{:S(2)}, u32[]{:S(2)}) async-start(bf16[32,2,4,128,128]{4,3,2,1,0:T(8,128)(2,1)} %bitcast.15), calls=%async_computation.1 | async-start | bytes 16777216 | tf_op jit(solution)/shard_map/all_to_all | solution.py:319
  40.0 0.0 all-gather.2.cloned.1.call-start
  40.1 0.7 all-gather.2.cloned.1.call-update
  40.8 36.6 %all-gather.2.cloned.1.call-done.cot_ref = bf16[1024,1024]{1,0:T(8,128)(2,1)} async-done(((bf16[1024,256]{1,0:T(8,128)(2,1)}), bf16[1024,1024]{1,0:T(8,128)(2,1)}) %all-gather.2.cloned.1.call-update) | async-done | bytes 2097168 | tf_op jit(solution)/shard_map/all_gather | solution.py:340
  77.4 62.4 %all-to-all-done.1 = bf16[32,2,4,128,128]{4,3,2,1,0:T(8,128)(2,1)} async-done(((bf16[32,2,4,128,128]{4,3,2,1,0:T(8,128)(2,1)}), bf16[32,2,4,128,128]{4,3,2,1,0:T(8,128)(2,1)}, u32[]{:S(2)}, u32[]{:S(2)}) %all-to-all-start.1) | async-done | bytes 8388640 | tf_op jit(solution)/shard_map/all_to_all | solution.py:319
  139.8 53.1 %shard_map.95 = (bf16[1024,1024]{1,0:T(8,128)(2,1)}, f32[8,4,128,128]{3,2,1,0:T(8,128)}, bf16[64,4,128,128]{3,2,1,0:T(8,128)(2,1)}, bf16[1024,256]{1,0:T(8,128)(...) custom-call(s32[8,9]{1,0:T(8,128)} %entries_ref.1, bf16[1024,256]{1,0:T(8,128)(2,1)} %get-tuple-element.18.q_ref, ...), custom_call_target="tpu_custom_call" | custom-call | tf_op jit(solution)/shard_map/pallas_call | solution.py:187
  192.9 11.0 %all-to-all-start.2 = ((bf16[32,2,4,128,128]{4,3,2,1,0:T(8,128)(2,1)}), bf16[32,2,4,128,128]{4,3,2,1,0:T(8,128)(2,1)}, u32[]{:S(2)}, u32[]{:S(2)}) async-start(bf16[32,2,4,128,128]{4,3,2,1,0:T(8,128)(2,1)} %bitcast.16), calls=%async_computation.3 | async-start | bytes 16777216 | tf_op jit(solution)/shard_map/all_to_all | solution.py:319
  203.9 0.0 reduce-scatter.3.cloned.1.call-start
  203.9 0.7 reduce-scatter.3.cloned.1.call-update
  204.6 0.0 reduce-scatter.5.cloned.1.call-start
  204.7 99.0 %all-to-all-done.2 = bf16[32,2,4,128,128]{4,3,2,1,0:T(8,128)(2,1)} async-done(((bf16[32,2,4,128,128]{4,3,2,1,0:T(8,128)(2,1)}), bf16[32,2,4,128,128]{4,3,2,1,0:T(8,128)(2,1)}, u32[]{:S(2)}, u32[]{:S(2)}) %all-to-all-start.2) | async-done | bytes 8388640 | tf_op jit(solution)/shard_map/all_to_all | solution.py:319
  303.7 8.6 %shard_map.96.grad_kv_ref = bf16[8,4,128,128]{3,2,1,0:T(8,128)(2,1)} custom-call(s32[64]{0:T(128)} %reshape.39.wanted_ref, f32[8,4,128,128]{3,2,1,0:T(8,128)} %get-tuple-element.24.near_ref, bf16[64,4,128,128]{3,2,1,0:T(8,128)(2,1)} %bitcast.5.back_ref), custom_call_target="tpu_custom_call" | custom-call | tf_op jit(solution)/shard_map/pallas_call | solution.py:248
  312.3 8.5 %shard_map.97 = (bf16[1024,1024]{1,0:T(8,128)(2,1)}, f32[1024,2]{1,0:T(8,128)}, bf16[1024,512]{1,0:T(8,128)(2,1)}) custom-call(bf16[1024,1024]{1,0:T(8,128)(2,1)} %tokens_ref.3, bf16[1024,256]{1,0:T(8,128)(2,1)} %get-tuple-element.23.dq_ref, bf16[8,4,128,128]{3,2,1,0:T(8,128)(2,1)} %shard_map.96.grad_kv_ref, bf16[3,1024,256]{2,1,0:T(8,128)(2,1)} %bitcast.18), custom_call_target="tpu_custom_call" | custom-call | tf_op jit(solution)/shard_map/pallas_call | solution.py:294
  320.8 0.0 copy-start.2
  320.8 0.0 copy-start.1
  320.8 0.0 reduce-scatter.5.cloned.1.call-update
  320.8 1.2 copy-done.2
  322.0 0.1 convert.8
  322.1 0.3 copy-done.1
  322.3 0.1 convert.9
  322.4 0.1 pad_maximum_fusion
  322.5 0.0 copy-start.4
  322.5 0.0 copy-start.3
  322.5 26.5 %all_to_all.29 = bf16[32,32,512]{2,1,0:T(8,128)(2,1)S(1)} all-to-all(bf16[32,32,512]{2,1,0:T(8,128)(2,1)S(1)} %pad_maximum_fusion), channel_id=1, replica_groups=mesh['space'=32,'head'=4] {'space'}, dimensions={0} | all-to-all | bytes 2097152 | tf_op jit(solution)/shard_map/all_to_all | solution.py:319
  349.0 4.0 %all-to-all-start.4 = ((bf16[32,32,512]{2,1,0:T(8,128)(2,1)}), bf16[32,32,512]{2,1,0:T(8,128)(2,1)S(1)}, u32[]{:S(2)}, u32[]{:S(2)}) async-start(bf16[32,32,512]{2,1,0:T(8,128)(2,1)} %bitcast.8), calls=%async_computation.6 | async-start | bytes 2097152 | tf_op jit(solution)/shard_map/all_to_all | solution.py:319
  353.0 0.0 copy-done.4
  353.0 0.2 reduce.1
  353.3 0.0 copy-start.5
  353.3 0.0 copy-done.3
  353.3 0.2 reduce.3
  353.5 0.2 convert_reduce_fusion.1
  353.6 0.6 slice_bitcast_fusion
  354.3 0.0 copy-done.5
  354.3 0.0 copy-start
  354.3 19.4 %psum.7 = f32[1024,2]{1,0:T(8,128)S(1)} all-reduce(f32[1024,2]{1,0:T(8,128)S(1)} %copy-done.5), channel_id=1, replica_groups=mesh['space'=32,'head'=4] {'head'}, use_global_device_ids=true, to_apply=%region_2.0 | all-reduce | flops 2048 | bytes 16384 | tf_op jit(solution)/shard_map/psum | solution.py:355
  373.8 0.5 slice_reduce_fusion.1
  374.3 0.0 all-to-all-done.4
  374.3 0.2 convert_reduce_fusion
  374.5 0.6 copy.17
  375.1 0.0 reduce-scatter.3.cloned.1.call-done
  375.1 0.0 reduce-scatter.5.cloned.1.call-done
  375.1 0.0 copy-done
  375.1 2.7 fusion.6
  (2 shorter events, 0.0 us)
Async XLA Ops:
  8.5 16.3 %all-to-all-start = ((s32[32,1,2]{2,1,0:T(1,128)}), s32[32,1,2]{2,1,0:T(1,128)S(1)}, u32[]{:S(2)}, u32[]{:S(2)}) async-start(s32[32,1,2]{2,1,0:T(1,128)} %copy.13), calls=%async_computation | async-start | bytes 32768 | tf_op jit(solution)/shard_map/all_to_all | solution.py:319
  33.2 106.6 %all-to-all-start.1 = ((bf16[32,2,4,128,128]{4,3,2,1,0:T(8,128)(2,1)}), bf16[32,2,4,128,128]{4,3,2,1,0:T(8,128)(2,1)}, u32[]{:S(2)}, u32[]{:S(2)}) async-start(bf16[32,2,4,128,128]{4,3,2,1,0:T(8,128)(2,1)} %bitcast.15), calls=%async_computation.1 | async-start | bytes 16777216 | tf_op jit(solution)/shard_map/all_to_all | solution.py:319
  40.0 37.3 %all-gather.2.cloned.1.call-start = ((), (), s32[]{:S(2)}) async-start(), calls=%async_computation.7 | async-start | bytes 2621440 | tf_op jit(solution)/shard_map/all_gather | solution.py:340
  192.9 110.8 %all-to-all-start.2 = ((bf16[32,2,4,128,128]{4,3,2,1,0:T(8,128)(2,1)}), bf16[32,2,4,128,128]{4,3,2,1,0:T(8,128)(2,1)}, u32[]{:S(2)}, u32[]{:S(2)}) async-start(bf16[32,2,4,128,128]{4,3,2,1,0:T(8,128)(2,1)} %bitcast.16), calls=%async_computation.3 | async-start | bytes 16777216 | tf_op jit(solution)/shard_map/all_to_all | solution.py:319
  203.9 171.2 %reduce-scatter.3.cloned.1.call-start = ((), (), s32[]{:S(2)}) async-start(), calls=%async_computation.8 | async-start | bytes 2621440 | tf_op jit(solution)/shard_map/reduce_scatter | solution.py:349
  204.6 170.5 %reduce-scatter.5.cloned.1.call-start = ((), (), s32[]{:S(2)}) async-start(), calls=%async_computation.9 | async-start | bytes 2621440 | tf_op jit(solution)/shard_map/reduce_scatter | solution.py:354
  320.8 1.2 copy-start.2
  320.8 1.5 copy-start.1
  322.5 30.6 %copy-start.4 = (f32[1024,1]{1,0:T(8,128)S(1)}, f32[1024,1]{1,0:T(8,128)}, u32[]{:S(2)}) copy-start(f32[1024,1]{1,0:T(8,128)} %get-tuple-element.22) | copy-start | bytes 12292
  322.5 30.8 %copy-start.3 = (f32[1024,1]{1,0:T(8,128)S(1)}, f32[1024,1]{1,0:T(8,128)}, u32[]{:S(2)}) copy-start(f32[1024,1]{1,0:T(8,128)} %get-tuple-element.28) | copy-start | bytes 12292
  349.0 25.3 %all-to-all-start.4 = ((bf16[32,32,512]{2,1,0:T(8,128)(2,1)}), bf16[32,32,512]{2,1,0:T(8,128)(2,1)S(1)}, u32[]{:S(2)}, u32[]{:S(2)}) async-start(bf16[32,32,512]{2,1,0:T(8,128)(2,1)} %bitcast.8), calls=%async_computation.6 | async-start | bytes 2097152 | tf_op jit(solution)/shard_map/all_to_all | solution.py:319
  353.3 1.0 copy-start.5
  354.3 20.8 %copy-start = (bf16[1024,256]{1,0:T(8,128)(2,1)S(1)}, bf16[1024,256]{1,0:T(8,128)(2,1)}, u32[]{:S(2)}) copy-start(bf16[1024,256]{1,0:T(8,128)(2,1)} %param.11) | copy-start | bytes 1572868
Sparse Core Ops, SparseCore 0:
  42.5 34.7 all-gather.1
  207.1 30.9 reduce-scatter.2
  321.0 32.3 reduce-scatter.4

commit v2 on v1

--- a/solution.py
+++ b/solution.py
@@ -10,6 +10,7 @@
 HEAD_DIM = 64
 NEIGHBOURS = 9
 NEAR = 4
+REACHES = (1, 4)
 EPSILON = 1e-05
 F32 = jnp.float32
 BF16 = jnp.bfloat16
@@ -77,32 +78,188 @@
     )(tokens, w3)
 
 
-def pick_kernel(wanted_ref, kv_ref, out_ref):
-    first = pl.program_id(0) * out_ref.shape[0]
-    for i in range(out_ref.shape[0]):
-        out_ref[i] = kv_ref[jnp.maximum(wanted_ref[first + i], 0)]
-
-
-def pick_tiles(wanted, kv):
-    count = wanted.shape[0]
-    step = 8
+def copy_to(src, dst, sems, index, device):
+    return pltpu.make_async_remote_copy(
+        src_ref=src,
+        dst_ref=dst,
+        send_sem=sems.at[0, index],
+        recv_sem=sems.at[1, index],
+        device_id=device,
+        device_id_type=pl.DeviceIdType.MESH,
+    )
+
+
+def greet(peers, groups):
+    barrier = pltpu.get_barrier_semaphore()
+    me, group = lax.axis_index("space"), lax.axis_index("head")
+
+    @pl.loop(1, peers)
+    def _(r):
+        pl.semaphore_signal(
+            barrier,
+            inc=1,
+            device_id={"space": lax.rem(me + r, peers)},
+            device_id_type=pl.DeviceIdType.MESH,
+        )
+
+    for k in range(1, groups):
+        pl.semaphore_signal(
+            barrier,
+            inc=1,
+            device_id={"head": lax.rem(group + k, groups)},
+            device_id_type=pl.DeviceIdType.MESH,
+        )
+    pl.semaphore_wait(barrier, peers + groups - 2)
+
+
+def slot_ranges(peers, reach):
+    if 2 * reach >= peers - 1:
+        return [(1, peers, True)]
+    return [(1, reach + 1, True), (peers - reach, peers, True), (reach + 1, peers - reach, False)]
+
+
+def fetch_kernel(peers, groups, reach, wanted_ref, kv_ref, cot_ref, out_ref, cots_ref, staged, sems, row_sems, own_sem):
+    me, group = lax.axis_index("space"), lax.axis_index("head")
+    greet(peers, groups)
+    own = pltpu.make_async_copy(cot_ref, cots_ref.at[group], own_sem)
+    own.start()
+
+    def across(k):
+        return copy_to(
+            cot_ref, cots_ref.at[group], row_sems, k, {"head": lax.rem(group + k, groups)}
+        )
+
+    def along(r, wide):
+        peer = lax.rem(me + r, peers)
+        if wide:
+            return copy_to(staged.at[r], out_ref.at[me], sems, r, {"space": peer})
+        return copy_to(staged.at[r, 0], out_ref.at[me, 0], sems, r, {"space": peer})
+
+    for k in range(1, groups):
+        across(k).start()
+    slots = staged.shape[1]
+    for low, high, wide in slot_ranges(peers, reach):
+
+        @pl.loop(low, high)
+        def _(r, wide=wide):
+            peer = lax.rem(me + r, peers)
+            for c in range(slots if wide else 1):
+                staged[r, c] = kv_ref[jnp.maximum(wanted_ref[peer * slots + c], 0)]
+            along(r, wide).start()
+
+    for low, high, wide in slot_ranges(peers, reach):
+
+        @pl.loop(low, high)
+        def _(r, wide=wide):
+            along(r, wide).wait()
+
+    for k in range(1, groups):
+        across(k).wait()
+    own.wait()
+
+
+def fetch(wanted, kv, cot, peers, groups, reach, number):
+    slots = wanted.shape[0] // peers
+    out = (peers, slots) + kv.shape[1:]
+    whole = pl.BlockSpec(memory_space=pl.ANY)
     return pl.pallas_call(
-        pick_kernel,
-        grid_spec=pltpu.PrefetchScalarGridSpec(
-            num_scalar_prefetch=1,
-            grid=(count // step,),
-            in_specs=[pl.BlockSpec(kv.shape, lambda i, wanted: (0, 0, 0, 0))],
-            out_specs=pl.BlockSpec((step,) + kv.shape[1:], lambda i, wanted: (i, 0, 0, 0)),
+        functools.partial(fetch_kernel, peers, groups, reach),
+        in_specs=[
+            pl.BlockSpec(memory_space=pltpu.SMEM),
+            pl.BlockSpec(memory_space=pltpu.VMEM),
+            whole,
+        ],
+        out_specs=[whole, whole],
+        out_shape=[
+            jax.ShapeDtypeStruct(out, kv.dtype),
+            jax.ShapeDtypeStruct((groups,) + cot.shape, cot.dtype),
+        ],
+        scratch_shapes=[
+            pltpu.VMEM(out, kv.dtype),
+            pltpu.SemaphoreType.DMA((2, peers)),
+            pltpu.SemaphoreType.DMA((2, groups)),
+            pltpu.SemaphoreType.DMA,
+        ],
+        compiler_params=pltpu.CompilerParams(
+            collective_id=number, has_side_effects=True, vmem_limit_bytes=VMEM_BYTES
         ),
-        out_shape=jax.ShapeDtypeStruct((count,) + kv.shape[1:], kv.dtype),
-        compiler_params=pltpu.CompilerParams(vmem_limit_bytes=VMEM_BYTES),
-    )(wanted, kv)
+    )(wanted, kv, cot)
+
+
+def swap_kernel(peers, groups, reach, spaces, heads, slotted, *refs):
+    me, group = lax.axis_index("space"), lax.axis_index("head")
+    count = spaces + heads + slotted
+    sources, targets = refs[:count], refs[count : 2 * count]
+    sems, head_sems, own_sems = refs[2 * count :]
+    greet(peers, groups)
+    owns = []
+    for i in range(slotted, count):
+        at = me if i < slotted + spaces else group
+        owns.append(pltpu.make_async_copy(sources[i].at[at], targets[i].at[at], own_sems.at[i]))
+        owns[-1].start()
+
+    def across(i, k):
+        peer = lax.rem(group + k, groups)
+        return copy_to(
+            sources[i].at[peer], targets[i].at[group], head_sems.at[i], k, {"head": peer}
+        )
+
+    def along(i, r, wide):
+        peer = lax.rem(me + r, peers)
+        src, dst = sources[i].at[peer], targets[i].at[me]
+        if not wide:
+            src, dst = sources[i].at[peer, 0], targets[i].at[me, 0]
+        return copy_to(src, dst, sems.at[i], r, {"space": peer})
+
+    def each(act):
+        for i in range(slotted, slotted + spaces):
+
+            @pl.loop(1, peers)
+            def _(r, i=i):
+                act(along(i, r, True))
+
+        for i in range(slotted):
+            for low, high, wide in slot_ranges(peers, reach):
+
+                @pl.loop(low, high)
+                def _(r, i=i, wide=wide):
+                    act(along(i, r, wide))
+
+    for i in range(slotted + spaces, count):
+        for k in range(1, groups):
+            across(i, k).start()
+    each(lambda copy: copy.start())
+    each(lambda copy: copy.wait())
+    for i in range(slotted + spaces, count):
+        for k in range(1, groups):
+            across(i, k).wait()
+    for own in owns:
+        own.wait()
+
+
+def swap(slotted, spaces, heads, peers, groups, reach, number):
+    arrays = (*slotted, *spaces, *heads)
+    whole = pl.BlockSpec(memory_space=pl.ANY)
+    return pl.pallas_call(
+        functools.partial(
+            swap_kernel, peers, groups, reach, len(spaces), len(heads), len(slotted)
+        ),
+        in_specs=[whole] * len(arrays),
+        out_specs=[whole] * len(arrays),
+        out_shape=[jax.ShapeDtypeStruct(a.shape, a.dtype) for a in arrays],
+        scratch_shapes=[
+            pltpu.SemaphoreType.DMA((len(arrays), 2, peers)),
+            pltpu.SemaphoreType.DMA((len(arrays), 2, groups)),
+            pltpu.SemaphoreType.DMA((len(arrays),)),
+        ],
+        compiler_params=pltpu.CompilerParams(collective_id=number, has_side_effects=True),
+    )(*arrays)
 
 
 def attention_kernel(entries_ref, q_ref, cot_ref, w_out_ref, normed_ref, *refs):
     kv_refs = refs[:NEIGHBOURS]
-    att_out_ref, near_ref, far_ref, dq_ref, grad_out_ref, grad_q_ref = refs[NEIGHBOURS:-2]
-    far_total, held = refs[-2:]
+    att_out_ref, near_ref, far_ref, dq_ref, early_ref = refs[NEIGHBOURS:-4]
+    far_total, held, grad_out, grad_q = refs[-4:]
     tile = pl.program_id(0)
     last = pl.num_programs(0) - 1
     heads = q_ref.shape[1] // HEAD_DIM
@@ -111,14 +268,16 @@
     @pl.when(tile == 0)
     def _():
         near_ref[...] = jnp.zeros_like(near_ref)
-        grad_out_ref[...] = jnp.zeros_like(grad_out_ref)
-        grad_q_ref[...] = jnp.zeros_like(grad_q_ref)
+        grad_out[...] = jnp.zeros_like(grad_out)
+        grad_q[...] = jnp.zeros_like(grad_q)
 
         @pl.loop(0, far_total.shape[0])
         def _(i):
             far_total[i] = jnp.zeros(far_total.shape[1:], F32)
 
-    cot = cot_ref[...]
+    groups = cot_ref.shape[0]
+    share = cot_ref.shape[2]
+    cot = jnp.concatenate([cot_ref[g] for g in range(groups)], 1)
     grad_attended = dot(cot, w_out_ref[...], ((1,), (1,))).astype(BF16)
     q = q_ref[...]
     left = lax.broadcasted_iota(jnp.int32, (128, 128), 1) < HEAD_DIM
@@ -156,9 +315,11 @@
     dq = (dq_t.T * HEAD_DIM ** (-0.5)).astype(BF16)
     attended = att_t.T.astype(BF16)
     dq_ref[...] = dq
-    att_out_ref[...] = dot(attended, w_out_ref[...], ((1,), (0,))).astype(BF16)
-    grad_out_ref[...] += dot(cot, attended, ((0,), (0,)))
-    grad_q_ref[...] += dot(normed_ref[...], dq, ((0,), (0,)))
+    att_out = dot(attended, w_out_ref[...], ((1,), (0,))).astype(BF16)
+    for g in range(groups):
+        att_out_ref[g] = att_out[:, g * share : (g + 1) * share]
+    grad_out[...] += dot(cot, attended, ((0,), (0,)))
+    grad_q[...] += dot(normed_ref[...], dq, ((0,), (0,)))
 
     @pl.when(tile == last)
     def _():
@@ -166,13 +327,19 @@
         def _(i):
             far_ref[i] = far_total[i].astype(BF16)
 
+        cols = grad_q.shape[1]
+        early_ref[:, :cols] = grad_out[...].astype(BF16)
+        early_ref[:, cols:] = grad_q[...].astype(BF16)
+
 
 def attention(entries, q, cot, w_out, normed, kv, fetched):
     tiles, heads, rows, mixed = kv.shape
     slots = fetched.shape[0]
     tile_block = (1, heads, rows, mixed)
     cols = q.shape[1]
-    width = cot.shape[1]
+    groups, _, share = cot.shape
+    width = groups * share
+    cot_spec = pl.BlockSpec((groups, rows, share), lambda t, e: (0, t, 0))
     whole2 = lambda t, e: (0, 0)
     row2 = lambda t, e: (t, 0)
     kv_specs = []
@@ -191,33 +358,33 @@
             grid=(tiles,),
             in_specs=[
                 pl.BlockSpec((rows, cols), row2),
-                pl.BlockSpec((rows, width), row2),
+                cot_spec,
                 pl.BlockSpec((cols, width), whole2),
                 pl.BlockSpec((rows, width), row2),
             ]
             + kv_specs,
             out_specs=[
-                pl.BlockSpec((rows, width), row2),
+                cot_spec,
                 pl.BlockSpec(kv.shape, lambda t, e: (0, 0, 0, 0), pipeline_mode=once),
                 pl.BlockSpec(fetched.shape, lambda t, e: (0, 0, 0, 0), pipeline_mode=once),
                 pl.BlockSpec((rows, cols), row2),
-                pl.BlockSpec((width, cols), whole2, pipeline_mode=once),
-                pl.BlockSpec((width, cols), whole2, pipeline_mode=once),
+                pl.BlockSpec((width, 2 * cols), whole2, pipeline_mode=once),
             ],
             scratch_shapes=[
                 pltpu.VMEM(fetched.shape, F32),
                 pltpu.VMEM((NEIGHBOURS,) + kv.shape[1:], F32),
+                pltpu.VMEM((width, cols), F32),
+                pltpu.VMEM((width, cols), F32),
             ],
         ),
         out_shape=[
-            jax.ShapeDtypeStruct((tiles * rows, width), BF16),
+            jax.ShapeDtypeStruct(cot.shape, BF16),
             jax.ShapeDtypeStruct(kv.shape, F32),
             jax.ShapeDtypeStruct(fetched.shape, BF16),
             jax.ShapeDtypeStruct((tiles * rows, cols), BF16),
-            jax.ShapeDtypeStruct((width, cols), F32),
-            jax.ShapeDtypeStruct((width, cols), F32),
-        ],
-        compiler_params=pltpu.CompilerParams(vmem_limit_bytes=VMEM_BYTES),
+            jax.ShapeDtypeStruct((width, 2 * cols), BF16),
+        ],
+        compiler_params=pltpu.CompilerParams(vmem_limit_bytes=50 * 2**20),
     )(entries, q, cot, w_out, normed, *([kv] * NEAR + [fetched] * (NEIGHBOURS - NEAR)))
 
 
@@ -278,15 +445,17 @@
     part += dot(dk, w_ref[1], ((1,), (1,)))
     part += dot(dv, w_ref[2], ((1,), (1,)))
     sums = [jnp.sum(part, 1, keepdims=True), jnp.sum(part * standard, 1, keepdims=True)]
-    sums_ref[...] = jnp.concatenate(sums, 1)
-    part_ref[...] = part.astype(BF16)
+    sums_ref[...] = jnp.concatenate(sums, 1).T
+    share = part_ref.shape[2]
+    for g in range(part_ref.shape[0]):
+        part_ref[g] = part[:, g * share : (g + 1) * share].astype(BF16)
 
     @pl.when(step == pl.num_programs(0) - 1)
     def _():
         grad_w_ref[...] = total[...].astype(BF16)
 
 
-def finish(tokens, dq, grad_kv, w3):
+def finish(tokens, dq, grad_kv, w3, groups):
     rows, width = tokens.shape
     cols = dq.shape[1]
     step = 256
@@ -301,28 +470,18 @@
             pl.BlockSpec((3, width, cols), lambda i: (0, 0, 0)),
         ],
         out_specs=[
-            pl.BlockSpec((step, width), row2),
-            pl.BlockSpec((step, 2), row2),
+            pl.BlockSpec((groups, step, width // groups), lambda i: (0, i, 0)),
+            pl.BlockSpec((2, step), lambda i: (0, i)),
             pl.BlockSpec((width, 2 * cols), lambda i: (0, 0)),
         ],
         out_shape=[
-            jax.ShapeDtypeStruct((rows, width), BF16),
-            jax.ShapeDtypeStruct((rows, 2), F32),
+            jax.ShapeDtypeStruct((groups, rows, width // groups), BF16),
+            jax.ShapeDtypeStruct((2, rows), F32),
             jax.ShapeDtypeStruct((width, 2 * cols), BF16),
         ],
         scratch_shapes=[pltpu.VMEM((width, 2 * cols), F32)],
         compiler_params=pltpu.CompilerParams(vmem_limit_bytes=VMEM_BYTES),
     )(tokens, dq, grad_kv, w3)
-
-
-def exchange(array):
-    return lax.all_to_all(array, "space", split_axis=0, concat_axis=0, tiled=True)
-
-
-def sum_rows(part, peers):
-    width, cols = part.shape
-    arrived = exchange(part.reshape(peers, width // peers, cols))
-    return jnp.sum(arrived.astype(F32), 0)
 
 
 def on_device(tokens, w_qkv, w_out, neighbours, requests, cotangent):
@@ -330,36 +489,64 @@
     tiles = neighbours.shape[0]
     rows = row_count // tiles
     cols = w_qkv.shape[2]
-    peers = lax.axis_size("space")
-    slot_count = requests.shape[2]
+    peers, groups = lax.axis_size("space"), lax.axis_size("head")
     share = cotangent.shape[1]
+    me = lax.axis_index("space")
     column = lax.axis_index("head") * share
     w3 = jnp.transpose(w_qkv, (1, 0, 2))
 
-    incoming = exchange(requests.reshape(peers, slot_count)).reshape(-1)
-    cot_full = lax.all_gather(cotangent, "head", axis=1, tiled=True)
+    table = lax.all_gather(requests[0], "space")
+    wanted = lax.dynamic_index_in_dim(table, me, 1, keepdims=False).reshape(-1)
+    apart = jnp.abs(jnp.arange(peers)[:, None] - jnp.arange(peers)[None, :])
+    apart = jnp.minimum(apart, peers - apart)
+    reach = jnp.max(jnp.where(jnp.any(table[:, :, 1:] >= 0, axis=2), apart, 0))
+    level = (reach > REACHES[0]).astype(jnp.int32) + (reach > REACHES[1]).astype(jnp.int32)
+    reaches = (*REACHES, peers)
+
     normed, q, kv, mean, inverse = project(tokens, w3, rows)
-    outgoing = pick_tiles(incoming, kv)
-    fetched = exchange(outgoing.reshape((peers, slot_count) + kv.shape[1:]))
-    fetched = fetched.reshape(outgoing.shape)
-    att_out, near, far, dq, grad_out, grad_q = attention(
-        neighbours, q, cot_full, w_out, normed, kv, fetched
+    fetched, cots = lax.switch(
+        level,
+        [
+            functools.partial(fetch, peers=peers, groups=groups, reach=r, number=n)
+            for n, r in enumerate(reaches)
+        ],
+        wanted,
+        kv,
+        cotangent,
     )
-    back = exchange(far.reshape((peers, slot_count) + kv.shape[1:]))
-    summed = lax.psum_scatter(att_out, "head", scatter_dimension=1, tiled=True)
-    early = sum_rows(jnp.concatenate([grad_out, grad_q], 1).astype(BF16), peers)
-    grad_kv = place(incoming, near, back.reshape(outgoing.shape))
-    part, sums, grad_w_kv = finish(tokens, dq, grad_kv, w3)
-    late = sum_rows(grad_w_kv, peers)
-    own_part = lax.psum_scatter(part, "head", scatter_dimension=1, tiled=True).astype(F32)
-    sums = lax.psum(sums, "head") / width
+    attended, near, far, dq, early = attention(
+        neighbours, q, cots, w_out, normed, kv, fetched.reshape((-1,) + kv.shape[1:])
+    )
+
+    def give_back(far, early, attended, reach, number):
+        return swap((far,), (early,), (attended,), peers, groups, reach, number)
+
+    back, early, attended = lax.switch(
+        level,
+        [
+            functools.partial(give_back, reach=r, number=n + len(reaches))
+            for n, r in enumerate(reaches)
+        ],
+        far.reshape(fetched.shape),
+        early.reshape(peers, width // peers, 2 * cols),
+        attended,
+    )
+    grad_kv = place(wanted, near, back.reshape(far.shape))
+    part, sums, late = finish(tokens, dq, grad_kv, w3, groups)
+    sums = jnp.broadcast_to(sums, (groups,) + sums.shape)
+    late = late.reshape(peers, width // peers, 2 * cols)
+    late, part, sums = swap((), (late,), (part, sums), peers, groups, peers, 2 * len(reaches))
 
     own_tokens = lax.dynamic_slice_in_dim(tokens, column, share, 1).astype(F32)
-    layer_out = (own_tokens + summed.astype(F32)).astype(BF16)
+    layer_out = (own_tokens + jnp.sum(attended.astype(F32), 0)).astype(BF16)
     own_standard = (own_tokens - mean) * inverse
+    own_part = jnp.sum(part.astype(F32), 0)
+    means = (jnp.sum(sums, 0) / width)[:, :, None]
     grad_tokens = (
-        cotangent.astype(F32) + inverse * (own_part - sums[:, :1] - own_standard * sums[:, 1:])
+        cotangent.astype(F32) + inverse * (own_part - means[0] - own_standard * means[1])
     ).astype(BF16)
+    early = jnp.sum(early.astype(F32), 0)
+    late = jnp.sum(late.astype(F32), 0)
     grad_w_qkv = jnp.concatenate([early[:, cols:], late], 1).reshape(-1, 3, cols)
     grad_w_out = early[:, :cols].T
     return (layer_out, grad_tokens, grad_w_qkv, grad_w_out)

time: 388 us -> 307 us (0.79)
  waiting for transfers between devices: 200 us -> 0 us
  Pallas kernels: 83 us -> 262 us
  starting transfers between devices: 31.4 us -> 0 us
  blocking collectives: 46 us -> 26.8 us
  between operations: 13.9 us -> 2.13 us
  other arithmetic: 4.34 us -> 9.25 us
    pallas_call x1 -> x3, Pallas kernels: 6.5 us -> 188 us  [the longest x2 115 us: swap(): pl.pallas_call(functools.partial(swap_kernel, peers, groups, reach, len(s...]
    all_to_all x4 -> x0, waiting for transfers between devices: 162 us -> none  [exchange(): lax.all_to_all(array, 'space', split_axis=0, concat_axis=0, tiled=True)]
    all_gather x1 -> x0, waiting for transfers between devices: 36.6 us -> none  [on_device(): cot_full = lax.all_gather(cotangent, 'head', axis=1, tiled=True)]
    all_to_all x4 -> x0, starting transfers between devices: 31.3 us -> none  [exchange(): lax.all_to_all(array, 'space', split_axis=0, concat_axis=0, tiled=True)]
    all_gather x0 -> x1, blocking collectives: none -> 26.8 us  [on_device(): table = lax.all_gather(requests[0], 'space')]
    all_to_all x1 -> x0, blocking collectives: 26.5 us -> none  [exchange(): lax.all_to_all(array, 'space', split_axis=0, concat_axis=0, tiled=True)]
    psum x1 -> x0, blocking collectives: 19.4 us -> none  [on_device(): sums = lax.psum(sums, 'head') / width]
  transfers between devices with their start and end apart: 7 -> 0, of which waited for: 4 -> 0; matrix products, arithmetic and copies ran while one was open for 1% -> 0% of each run, Pallas kernels for 6% -> 0%
where the time goes in v2:
time: 307 us; the launch traced here: 306 us
  Pallas kernels  262 us (85%)
  blocking collectives  26.8 us (9%)
  other arithmetic  9.25 us (3%)
  local copies, waits for them, and re-layouts  5.57 us (2%)
    pallas_call x2, Pallas kernels, swap(): pl.pallas_call(functools.partial(swap_kernel, peers, groups, reach, len(s...  115 us
    pallas_call x1, Pallas kernels, fetch(): pl.pallas_call(functools.partial(fetch_kernel, peers, groups, reach), in_...  73.7 us
    pallas_call x1, Pallas kernels, attention(): pl.pallas_call(attention_kernel, grid_spec=pltpu.PrefetchScalarGridSpec(n...  50.5 us
    all_gather x1, blocking collectives, on_device(): table = lax.all_gather(requests[0], 'space')  26.8 us
    pallas_call x1, Pallas kernels, finish(): pl.pallas_call(functools.partial(finish_kernel, cols // HEAD_DIM), grid=(...  8.54 us
    pallas_call x1, Pallas kernels, place(): pl.pallas_call(place_kernel, grid_spec=pltpu.PrefetchScalarGridSpec(num_s...  8.51 us
    pallas_call x1, Pallas kernels, project(): pl.pallas_call(functools.partial(project_kernel, cols // HEAD_DIM), grid=...  6.63 us

profile of v2, /device:TPU:1, one launch (start us, length us, event | category | flops | bytes accessed | tf_op | source)
XLA Modules:
  0.0 306.3 jit_solution(12237855831797495879)
XLA Ops:
  0.6 26.8 %all_gather.3 = s32[32,32,2]{1,2,0:T(2,128)S(1)} all-gather(s32[1,32,2]{1,2,0:T(2,128)} %param.16), channel_id=1, replica_groups=mesh['space'=32,'head'=4] {'space'}, dimensions={0}, use_global_device_ids=true | all-gather | bytes 8448 | tf_op jit(solution)/shard_map/all_gather | solution.py:498
  27.4 0.7 dynamic-slice_reduce_fusion
  28.2 0.1 reshape.41.wanted_ref
  28.3 0.6 fusion.8
  30.2 0.0 copy-start.5
  30.2 6.6 %shard_map.93 = (bf16[1024,1024]{1,0:T(8,128)(2,1)}, bf16[1024,256]{1,0:T(8,128)(2,1)}, bf16[8,4,128,128]{3,2,1,0:T(8,128)(2,1)S(1)}, f32[1024,1]{1,0:T(8,128)}, f32[1024,1]{1,0:T(8,128)}) custom-call(bf16[1024,1024]{1,0:T(8,128)(2,1)} %tokens_ref.3, bf16[3,1024,256]{2,1,0:T(8,128)(2,1)} %bitcast.29), custom_call_target="tpu_custom_call" | custom-call | tf_op jit(solution)/shard_map/pallas_call | solution.py:56
  36.9 1.2 reduce.1
  38.1 0.0 copy-done.5
  38.1 1.2 reduce.2
  39.4 0.0 copy-start.1
  39.4 0.0 copy-start.2
  39.4 0.0 copy-start.4
  39.4 73.7 %conditional.2 = (bf16[4,1024,256]{2,1,0:T(8,128)(2,1)}, bf16[64,4,128,128]{3,2,1,0:T(8,128)(2,1)}) conditional(s32[]{:T(128)} %clamp.4, (s32[64]{0:T(128)S(1)}, bf16[8,4,128,128]{3,2,1,0:T(8,128)(2,1)S(1)}, bf16[1024,256]{1,0:T(8,128)(2,1)S(1)}) %tuple.76, (s32[64]{0:T(128)S(1)}, bf16[8,4,128,128]{3,2,1,0:T(8,128)(2,1)S(1)}, ...), branch_computations={%region_1.2_spmd, %region_2.3_spmd, %region_3.4_spmd} | conditional | bytes 16 | solution.py:507
  39.4 73.7 %branch_0_fun.2 = (bf16[32,2,4,128,128]{4,3,2,1,0:T(8,128)(2,1)}, bf16[4,1024,256]{2,1,0:T(8,128)(2,1)}) custom-call(s32[64]{0:T(128)S(1)} %get-tuple-element.58.wanted_ref, bf16[8,4,128,128]{3,2,1,0:T(8,128)(2,1)S(1)} %get-tuple-element.59.kv_ref, bf16[1024,256]{1,0:T(8,128)(2,1)S(1)} %get-tuple-element.60.cot_ref), custom_call_target="tpu_custom_call" | custom-call | tf_op jit(solution)/shard_map/cond/branch_0_fun/pallas_call | solution.py:165
  113.1 0.0 copy-done.1
  113.1 0.0 copy-done.2
  113.1 0.0 copy-done.4
  113.1 50.5 %shard_map.94 = (bf16[4,1024,256]{2,1,0:T(8,128)(2,1)}, f32[8,4,128,128]{3,2,1,0:T(8,128)S(1)}, bf16[64,4,128,128]{3,2,1,0:T(8,128)(2,1)}, bf16[1024,256]{1,0:T(8,128)(2,1)S(1)}, bf16[1024,512]{1,0:T(8,128)(2,1)S(1)}) custom-call(s32[8,9]{1,0:T(8,128)S(1)} %copy-done.4, bf16[1024,256]{1,0:T(8,128)(2,1)S(1)} %copy-done.2, ...), custom_call_target="tpu_custom_call" | custom-call | tf_op jit(solution)/shard_map/pallas_call | solution.py:354
  163.6 0.0 copy-start
  163.6 1.3 copy-done
  164.9 0.0 copy-start.3
  164.9 0.8 copy-done.3
  165.7 84.2 %conditional.3 = ((bf16[32,2,4,128,128]{4,3,2,1,0:T(8,128)(2,1)}, bf16[32,32,512]{2,1,0:T(8,128)(2,1)S(1)}, bf16[4,1024,256]{2,1,0:T(8,128)(2,1)})) conditional(s32[]{:T(128)} %clamp.4, (bf16[32,2,4,128,128]{4,3,2,1,0:T(8,128)(2,1)}, bf16[32,32,512]{2,1,0:T(8,128)(2,1)S(1)}, bf16[4,1024,256]{2,1,0:T(8,128)(2,1)}) %tuple.73, ...), branch_computations={%region_4.5_spmd, %region_5.6_spmd, %region_6.7_spmd} | conditional | bytes 8 | solution.py:524
  165.7 84.1 %branch_0_fun.3 = (bf16[32,2,4,128,128]{4,3,2,1,0:T(8,128)(2,1)}, bf16[32,32,512]{2,1,0:T(8,128)(2,1)S(1)}, bf16[4,1024,256]{2,1,0:T(8,128)(2,1)}) custom-call(bf16[32,2,4,128,128]{4,3,2,1,0:T(8,128)(2,1)} %get-tuple-element.73.refs_0_, bf16[32,32,512]{2,1,0:T(8,128)(2,1)S(1)} %get-tuple-element.74.refs_1_, bf16[4,1024,256]{2,1,0:T(8,128)(2,1)} %get-tuple-element.75.refs_2_), custom_call_target="tpu_custom_call" | custom-call | tf_op jit(solution)/shard_map/cond/branch_0_fun/pallas_call | solution.py:243
  250.0 8.5 %shard_map.95.grad_kv_ref = bf16[8,4,128,128]{3,2,1,0:T(8,128)(2,1)} custom-call(s32[64]{0:T(128)S(1)} %reshape.41.wanted_ref, f32[8,4,128,128]{3,2,1,0:T(8,128)} %copy-done, bf16[64,4,128,128]{3,2,1,0:T(8,128)(2,1)} %bitcast.28), custom_call_target="tpu_custom_call" | custom-call | tf_op jit(solution)/shard_map/pallas_call | solution.py:415
  258.5 0.2 convert_reduce_fusion.3
  258.6 0.6 slice_bitcast_fusion
  259.2 8.5 %shard_map.96 = (bf16[4,1024,256]{2,1,0:T(8,128)(2,1)}, f32[2,1024]{1,0:T(2,128)}, bf16[1024,512]{1,0:T(8,128)(2,1)}) custom-call(bf16[1024,1024]{1,0:T(8,128)(2,1)} %tokens_ref.3, bf16[1024,256]{1,0:T(8,128)(2,1)} %copy-done.3, bf16[8,4,128,128]{3,2,1,0:T(8,128)(2,1)} %shard_map.95.grad_kv_ref, bf16[3,1024,256]{2,1,0:T(8,128)(2,1)} %bitcast.30), custom_call_target="tpu_custom_call" | custom-call | tf_op jit(solution)/shard_map/pallas_call | solution.py:463
  267.8 1.3 broadcast_in_dim.11.refs_2_
  269.1 30.5 %shard_map.97 = (bf16[32,32,512]{2,1,0:T(8,128)(2,1)}, bf16[4,1024,256]{2,1,0:T(8,128)(2,1)}, f32[4,2,1024]{2,1,0:T(2,128)}) custom-call(bf16[32,32,512]{2,1,0:T(8,128)(2,1)} %bitcast.31, bf16[4,1024,256]{2,1,0:T(8,128)(2,1)} %get-tuple-element.121.refs_1_, f32[4,2,1024]{2,1,0:T(2,128)} %broadcast_in_dim.11.refs_2_), custom_call_target="tpu_custom_call" | custom-call | tf_op jit(solution)/shard_map/pallas_call | solution.py:243
  299.6 0.0 copy-start.8
  299.6 0.0 copy-start.6
  299.6 3.1 %convert_reduce_fusion = (f32[1024,256]{1,0:T(8,128)S(1)}, f32[1024,256]{1,0:T(8,128)S(1)}) fusion(bf16[4,1024,256]{2,1,0:T(8,128)(2,1)} %get-tuple-element.148, bf16[4,1024,256]{2,1,0:T(8,128)(2,1)} %get-tuple-element.123), kind=kLoop, calls=%fused_computation | loop fusion | flops 3670016 | bytes 6291456 | tf_op jit(solution)/shard_map/reduce_sum | solution.py:541
  302.7 0.0 copy-done.8
  302.8 0.0 copy-done.6
  302.8 0.0 copy-start.7
  302.8 2.7 fusion.6
  305.5 0.0 copy-done.7
  305.5 0.2 convert_reduce_fusion.2
  305.6 0.6 copy.18
  (5 shorter events, 0.1 us)
Async XLA Ops:
  30.2 7.9 %copy-start.5 = (bf16[1024,256]{1,0:T(8,128)(2,1)S(1)}, bf16[1024,256]{1,0:T(8,128)(2,1)}, u32[]{:S(2)}) copy-start(bf16[1024,256]{1,0:T(8,128)(2,1)} %param.17) | copy-start | bytes 1572868
  39.4 73.7 %copy-start.1 = (bf16[256,1024]{1,0:T(8,128)(2,1)S(1)}, bf16[256,1024]{1,0:T(8,128)(2,1)}, u32[]{:S(2)}) copy-start(bf16[256,1024]{1,0:T(8,128)(2,1)} %w_out_ref.1) | copy-start | bytes 1572868
  39.4 73.7 %copy-start.2 = (bf16[1024,256]{1,0:T(8,128)(2,1)S(1)}, bf16[1024,256]{1,0:T(8,128)(2,1)}, u32[]{:S(2)}) copy-start(bf16[1024,256]{1,0:T(8,128)(2,1)} %get-tuple-element.107.q_ref) | copy-start | bytes 1572868
  39.4 73.7 %copy-start.4 = (s32[8,9]{1,0:T(8,128)S(1)}, s32[8,9]{1,0:T(8,128)}, u32[]{:S(2)}) copy-start(s32[8,9]{1,0:T(8,128)} %entries_ref.1) | copy-start | bytes 868
  163.6 1.3 copy-start
  164.9 0.8 copy-start.3
  299.6 3.1 %copy-start.8 = (f32[4,2,1024]{2,1,0:T(2,128)S(1)}, f32[4,2,1024]{2,1,0:T(2,128)}, u32[]{:S(2)}) copy-start(f32[4,2,1024]{2,1,0:T(2,128)} %get-tuple-element.124) | copy-start | bytes 98308
  299.6 3.2 %copy-start.6 = (bf16[1024,256]{1,0:T(8,128)(2,1)S(1)}, bf16[1024,256]{1,0:T(8,128)(2,1)}, u32[]{:S(2)}) copy-start(bf16[1024,256]{1,0:T(8,128)(2,1)} %param.17) | copy-start | bytes 1572868
  302.8 2.7 copy-start.7

commit v3 on v2

--- a/solution.py
+++ b/solution.py
@@ -11,6 +11,8 @@
 NEIGHBOURS = 9
 NEAR = 4
 REACHES = (1, 4)
+AT_ONCE = 2
+SLOTS = 2
 EPSILON = 1e-05
 F32 = jnp.float32
 BF16 = jnp.bfloat16
@@ -112,10 +114,28 @@
     pl.semaphore_wait(barrier, peers + groups - 2)
 
 
-def slot_ranges(peers, reach):
+def torus_order():
+    near = [(0, 1), (0, 3), (1, 0), (3, 0), (1, 1), (3, 3), (1, 3), (3, 1)]
+    far = [(0, 2), (2, 0), (1, 2), (2, 1), (3, 2), (2, 3), (2, 2)]
+    order = [(0, 0, 1)]
+    for group in (near[:4], near[4:], far[:2], far[2:6], far[6:]):
+        order += [(z, x, core) for core in (0, 1) for z, x in group]
+    return order
+
+
+ORDER = torus_order()
+
+
+def torus_peer(me, step):
+    z = lax.rem(me // 8 + step[0], 4)
+    x = lax.rem(lax.rem(me // 2, 4) + step[1], 4)
+    return z * 8 + x * 2 + lax.rem(lax.rem(me, 2) + step[2], 2)
+
+
+def second_ranges(peers, reach):
     if 2 * reach >= peers - 1:
-        return [(1, peers, True)]
-    return [(1, reach + 1, True), (peers - reach, peers, True), (reach + 1, peers - reach, False)]
+        return [(1, peers)]
+    return [(1, reach + 1), (peers - reach, peers)]
 
 
 def fetch_kernel(peers, groups, reach, wanted_ref, kv_ref, cot_ref, out_ref, cots_ref, staged, sems, row_sems, own_sem):
@@ -129,29 +149,34 @@
             cot_ref, cots_ref.at[group], row_sems, k, {"head": lax.rem(group + k, groups)}
         )
 
-    def along(r, wide):
-        peer = lax.rem(me + r, peers)
-        if wide:
-            return copy_to(staged.at[r], out_ref.at[me], sems, r, {"space": peer})
-        return copy_to(staged.at[r, 0], out_ref.at[me, 0], sems, r, {"space": peer})
+    def along(c, r, peer):
+        return copy_to(
+            staged.at[r, c], out_ref.at[me, c], sems, c * peers + r, {"space": peer}
+        )
 
     for k in range(1, groups):
         across(k).start()
-    slots = staged.shape[1]
-    for low, high, wide in slot_ranges(peers, reach):
+    for i, step in enumerate(ORDER):
+        peer = torus_peer(me, step)
+        staged[i, 0] = kv_ref[jnp.maximum(wanted_ref[peer * SLOTS], 0)]
+        along(0, i, peer).start()
+    for low, high in second_ranges(peers, reach):
 
         @pl.loop(low, high)
-        def _(r, wide=wide):
+        def _(r):
             peer = lax.rem(me + r, peers)
-            for c in range(slots if wide else 1):
-                staged[r, c] = kv_ref[jnp.maximum(wanted_ref[peer * slots + c], 0)]
-            along(r, wide).start()
-
-    for low, high, wide in slot_ranges(peers, reach):
+            staged[r, 1] = kv_ref[jnp.maximum(wanted_ref[peer * SLOTS + 1], 0)]
+            along(1, r, peer).start()
+
+    @pl.loop(0, len(ORDER))
+    def _(i):
+        along(0, i, lax.rem(me + 1, peers)).wait()
+
+    for low, high in second_ranges(peers, reach):
 
         @pl.loop(low, high)
-        def _(r, wide=wide):
-            along(r, wide).wait()
+        def _(r):
+            along(1, r, lax.rem(me + r, peers)).wait()
 
     for k in range(1, groups):
         across(k).wait()
@@ -159,8 +184,7 @@
 
 
 def fetch(wanted, kv, cot, peers, groups, reach, number):
-    slots = wanted.shape[0] // peers
-    out = (peers, slots) + kv.shape[1:]
+    out = (peers, SLOTS) + kv.shape[1:]
     whole = pl.BlockSpec(memory_space=pl.ANY)
     return pl.pallas_call(
         functools.partial(fetch_kernel, peers, groups, reach),
@@ -176,7 +200,7 @@
         ],
         scratch_shapes=[
             pltpu.VMEM(out, kv.dtype),
-            pltpu.SemaphoreType.DMA((2, peers)),
+            pltpu.SemaphoreType.DMA((2, SLOTS * peers)),
             pltpu.SemaphoreType.DMA((2, groups)),
             pltpu.SemaphoreType.DMA,
         ],
@@ -204,32 +228,45 @@
             sources[i].at[peer], targets[i].at[group], head_sems.at[i], k, {"head": peer}
         )
 
-    def along(i, r, wide):
-        peer = lax.rem(me + r, peers)
-        src, dst = sources[i].at[peer], targets[i].at[me]
-        if not wide:
-            src, dst = sources[i].at[peer, 0], targets[i].at[me, 0]
-        return copy_to(src, dst, sems.at[i], r, {"space": peer})
-
-    def each(act):
-        for i in range(slotted, slotted + spaces):
-
-            @pl.loop(1, peers)
-            def _(r, i=i):
-                act(along(i, r, True))
-
-        for i in range(slotted):
-            for low, high, wide in slot_ranges(peers, reach):
-
-                @pl.loop(low, high)
-                def _(r, i=i, wide=wide):
-                    act(along(i, r, wide))
+    def whole(i, r, peer):
+        return copy_to(sources[i].at[peer], targets[i].at[me], sems.at[i], r, {"space": peer})
+
+    def along(i, c, r, peer):
+        src, dst = sources[i].at[peer, c], targets[i].at[me, c]
+        return copy_to(src, dst, sems.at[i], c * peers + r, {"space": peer})
 
     for i in range(slotted + spaces, count):
         for k in range(1, groups):
             across(i, k).start()
-    each(lambda copy: copy.start())
-    each(lambda copy: copy.wait())
+    for r, step in enumerate(ORDER):
+        peer = torus_peer(me, step)
+        for i in range(slotted):
+            along(i, 0, r, peer).start()
+        for i in range(slotted, slotted + spaces):
+            whole(i, r, peer).start()
+    for i in range(slotted):
+        for low, high in second_ranges(peers, reach):
+
+            @pl.loop(low, high)
+            def _(r, i=i):
+                along(i, 1, r, lax.rem(me + r, peers)).start()
+
+    beside = lax.rem(me + 1, peers)
+
+    @pl.loop(0, len(ORDER))
+    def _(r):
+        for i in range(slotted):
+            along(i, 0, r, beside).wait()
+        for i in range(slotted, slotted + spaces):
+            whole(i, r, beside).wait()
+
+    for i in range(slotted):
+        for low, high in second_ranges(peers, reach):
+
+            @pl.loop(low, high)
+            def _(r, i=i):
+                along(i, 1, r, lax.rem(me + r, peers)).wait()
+
     for i in range(slotted + spaces, count):
         for k in range(1, groups):
             across(i, k).wait()
@@ -248,7 +285,7 @@
         out_specs=[whole] * len(arrays),
         out_shape=[jax.ShapeDtypeStruct(a.shape, a.dtype) for a in arrays],
         scratch_shapes=[
-            pltpu.SemaphoreType.DMA((len(arrays), 2, peers)),
+            pltpu.SemaphoreType.DMA((len(arrays), 2, SLOTS * peers)),
             pltpu.SemaphoreType.DMA((len(arrays), 2, groups)),
             pltpu.SemaphoreType.DMA((len(arrays),)),
         ],
@@ -257,10 +294,11 @@
 
 
 def attention_kernel(entries_ref, q_ref, cot_ref, w_out_ref, normed_ref, *refs):
-    kv_refs = refs[:NEIGHBOURS]
-    att_out_ref, near_ref, far_ref, dq_ref, early_ref = refs[NEIGHBOURS:-4]
+    kv_refs = refs[: AT_ONCE * NEIGHBOURS]
+    att_out_ref, near_ref, far_ref, dq_ref, early_ref = refs[AT_ONCE * NEIGHBOURS : -4]
     far_total, held, grad_out, grad_q = refs[-4:]
     tile = pl.program_id(0)
+    rows = q_ref.shape[0] // AT_ONCE
     last = pl.num_programs(0) - 1
     heads = q_ref.shape[1] // HEAD_DIM
     own = near_ref.shape[0]
@@ -281,39 +319,59 @@
     grad_attended = dot(cot, w_out_ref[...], ((1,), (1,))).astype(BF16)
     q = q_ref[...]
     left = lax.broadcasted_iota(jnp.int32, (128, 128), 1) < HEAD_DIM
-    mixed_t = []
-    for h in range(heads):
-        cut = head_cut(h)
-        pair = jnp.concatenate([q[:, cut], grad_attended[:, cut]], 1)
+    upper = lax.broadcasted_iota(jnp.int32, (128, 128), 0) < HEAD_DIM
+
+    def begin(u, h):
+        span = slice(u * rows, (u + 1) * rows)
+        pair = jnp.concatenate([q[span, head_cut(h)], grad_attended[span, head_cut(h)]], 1)
+        pair_t = pair.T
         zero = jnp.zeros_like(pair)
         stacked = jnp.concatenate([jnp.where(left, pair, zero), jnp.where(left, zero, pair)], 0)
-        kv = jnp.concatenate([r[0, h] for r in kv_refs], 0)
-        both = dot(kv, stacked, ((1,), (1,)))
-        scores = both[:, :128]
-        grad_prob = both[:, 128:]
-        weights = jnp.exp(scores - jnp.max(scores, axis=0, keepdims=True))
-        inverse = 1.0 / jnp.sum(weights, axis=0, keepdims=True)
-        row_delta = jnp.sum(weights * grad_prob, axis=0, keepdims=True) * inverse
+        stacked_t = jnp.concatenate(
+            [jnp.where(upper, pair_t, zero), jnp.where(upper, zero, pair_t)], 1
+        )
+        mine = kv_refs[u * NEIGHBOURS : (u + 1) * NEIGHBOURS]
+        kv = jnp.concatenate([r[0, h] for r in mine], 0)
+        return stacked_t, kv, dot(stacked, kv, ((1,), (1,)))
+
+    mixed = []
+    order = [(u, h) for u in range(AT_ONCE) for h in range(heads)]
+    following = begin(*order[0])
+    for at, (u, h) in enumerate(order):
+        stacked_t, kv, both = following
+        if at + 1 < len(order):
+            following = begin(*order[at + 1])
+        scores = both[:128]
+        grad_prob = both[128:]
+        weights = jnp.exp(scores - jnp.max(scores, axis=1, keepdims=True))
+        inverse = 1.0 / jnp.sum(weights, axis=1, keepdims=True)
+        row_delta = jnp.sum(weights * grad_prob, axis=1, keepdims=True) * inverse
         likely = weights * inverse
         grad_score = likely * (grad_prob - row_delta)
-        factors = jnp.concatenate([grad_score.astype(BF16), likely.astype(BF16)], 1)
-        grad_kv = dot(factors, stacked, ((1,), (0,)))
+        factors = jnp.concatenate([grad_score.astype(BF16), likely.astype(BF16)], 0)
+        mixed.append(dot(factors, kv, ((1,), (0,))))
+        grad_kv_t = dot(stacked_t, factors, ((1,), (0,)))
         for j in range(NEIGHBOURS):
-            held[j, h] = grad_kv[j * 128 : (j + 1) * 128]
-        mixed_t.append(dot(kv, factors, ((0,), (0,))))
-
-    @pl.loop(0, NEAR)
-    def _(j):
-        near_ref[entries_ref[tile, j]] += held[j]
-
-    @pl.loop(NEAR, NEIGHBOURS)
-    def _(j):
-        far_total[entries_ref[tile, j] - own] += held[j]
-
-    dq_t = jnp.concatenate([m[:HEAD_DIM, :128] for m in mixed_t], 0)
-    att_t = jnp.concatenate([m[HEAD_DIM:, 128:] for m in mixed_t], 0)
-    dq = (dq_t.T * HEAD_DIM ** (-0.5)).astype(BF16)
-    attended = att_t.T.astype(BF16)
+            held[u * NEIGHBOURS + j, h] = grad_kv_t[:, j * 128 : (j + 1) * 128]
+
+    for u in range(AT_ONCE):
+
+        @pl.loop(0, NEAR)
+        def _(j, u=u):
+            near_ref[entries_ref[tile * AT_ONCE + u, j]] += held[u * NEIGHBOURS + j]
+
+        @pl.loop(NEAR, NEIGHBOURS)
+        def _(j, u=u):
+            far_total[entries_ref[tile * AT_ONCE + u, j] - own] += held[u * NEIGHBOURS + j]
+
+
+    def join(parts):
+        lines = [jnp.concatenate(parts[i : i + heads], 1) for i in range(0, len(parts), heads)]
+        return jnp.concatenate(lines, 0)
+
+    dq = join([m[:128, :HEAD_DIM] for m in mixed])
+    dq = (dq * HEAD_DIM ** (-0.5)).astype(BF16)
+    attended = join([m[128:, HEAD_DIM:] for m in mixed]).astype(BF16)
     dq_ref[...] = dq
     att_out = dot(attended, w_out_ref[...], ((1,), (0,))).astype(BF16)
     for g in range(groups):
@@ -339,40 +397,43 @@
     cols = q.shape[1]
     groups, _, share = cot.shape
     width = groups * share
-    cot_spec = pl.BlockSpec((groups, rows, share), lambda t, e: (0, t, 0))
+    lines = AT_ONCE * rows
+    cot_spec = pl.BlockSpec((groups, lines, share), lambda t, e: (0, t, 0))
     whole2 = lambda t, e: (0, 0)
     row2 = lambda t, e: (t, 0)
     kv_specs = []
-    for j in range(NEIGHBOURS):
-        if j < NEAR:
-            kv_specs.append(pl.BlockSpec(tile_block, lambda t, e, j=j: (e[t, j], 0, 0, 0)))
-        else:
+    for u in range(AT_ONCE):
+        for j in range(NEIGHBOURS):
+            shift = 0 if j < NEAR else tiles
             kv_specs.append(
-                pl.BlockSpec(tile_block, lambda t, e, j=j: (e[t, j] - tiles, 0, 0, 0))
+                pl.BlockSpec(
+                    tile_block,
+                    lambda t, e, u=u, j=j, shift=shift: (e[t * AT_ONCE + u, j] - shift, 0, 0, 0),
+                )
             )
     once = pl.Buffered(1)
     return pl.pallas_call(
         attention_kernel,
         grid_spec=pltpu.PrefetchScalarGridSpec(
             num_scalar_prefetch=1,
-            grid=(tiles,),
+            grid=(tiles // AT_ONCE,),
             in_specs=[
-                pl.BlockSpec((rows, cols), row2),
+                pl.BlockSpec((lines, cols), row2),
                 cot_spec,
                 pl.BlockSpec((cols, width), whole2),
-                pl.BlockSpec((rows, width), row2),
+                pl.BlockSpec((lines, width), row2),
             ]
             + kv_specs,
             out_specs=[
                 cot_spec,
                 pl.BlockSpec(kv.shape, lambda t, e: (0, 0, 0, 0), pipeline_mode=once),
                 pl.BlockSpec(fetched.shape, lambda t, e: (0, 0, 0, 0), pipeline_mode=once),
-                pl.BlockSpec((rows, cols), row2),
+                pl.BlockSpec((lines, cols), row2),
                 pl.BlockSpec((width, 2 * cols), whole2, pipeline_mode=once),
             ],
             scratch_shapes=[
                 pltpu.VMEM(fetched.shape, F32),
-                pltpu.VMEM((NEIGHBOURS,) + kv.shape[1:], F32),
+                pltpu.VMEM((AT_ONCE * NEIGHBOURS,) + kv.shape[1:], F32),
                 pltpu.VMEM((width, cols), F32),
                 pltpu.VMEM((width, cols), F32),
             ],
@@ -385,7 +446,7 @@
             jax.ShapeDtypeStruct((width, 2 * cols), BF16),
         ],
         compiler_params=pltpu.CompilerParams(vmem_limit_bytes=50 * 2**20),
-    )(entries, q, cot, w_out, normed, *([kv] * NEAR + [fetched] * (NEIGHBOURS - NEAR)))
+    )(entries, q, cot, w_out, normed, *(([kv] * NEAR + [fetched] * (NEIGHBOURS - NEAR)) * AT_ONCE))
 
 
 def place_kernel(wanted_ref, near_ref, back_ref, grad_kv_ref, total):
@@ -437,7 +498,10 @@
         total[...] = jnp.zeros_like(total)
 
     standard, _, _ = norm_rows(tokens_ref[...])
-    pairs = [grad_kv_ref[:, h].reshape(standard.shape[0], 2 * HEAD_DIM) for h in range(heads)]
+    pairs = [
+        jnp.concatenate([grad_kv_ref[t, h].T for t in range(grad_kv_ref.shape[0])], 0)
+        for h in range(heads)
+    ]
     dk = jnp.concatenate([p[:, :HEAD_DIM] for p in pairs], 1)
     dv = jnp.concatenate([p[:, HEAD_DIM:] for p in pairs], 1)
     total[...] += dot(standard.astype(BF16), jnp.concatenate([dk, dv], 1), ((0,), (0,)))
@@ -495,7 +559,8 @@
     column = lax.axis_index("head") * share
     w3 = jnp.transpose(w_qkv, (1, 0, 2))
 
-    table = lax.all_gather(requests[0], "space")
+    copies = jnp.broadcast_to(requests, (peers,) + requests.shape[1:])
+    table = lax.all_to_all(copies, "space", split_axis=0, concat_axis=0, tiled=True)
     wanted = lax.dynamic_index_in_dim(table, me, 1, keepdims=False).reshape(-1)
     apart = jnp.abs(jnp.arange(peers)[:, None] - jnp.arange(peers)[None, :])
     apart = jnp.minimum(apart, peers - apart)

time: 307 us -> 260 us (0.85)
  Pallas kernels: 262 us -> 230 us
  blocking collectives: 26.8 us -> 0 us
  starting transfers between devices: 0 us -> 9.43 us
    all_gather x1 -> x0, blocking collectives: 26.8 us -> none  [on_device(): table = lax.all_gather(requests[0], 'space')]
    pallas_call x1, Pallas kernels: 50.5 us -> 33.1 us  [attention(): pl.pallas_call(attention_kernel, grid_spec=pltpu.PrefetchScalarGridSpec(n...]
    pallas_call x1, Pallas kernels: 73.7 us -> 59.7 us  [fetch(): pl.pallas_call(functools.partial(fetch_kernel, peers, groups, reach), in_...]
    all_to_all x0 -> x1, starting transfers between devices: none -> 9.43 us  [on_device(): lax.all_to_all(copies, 'space', split_axis=0, concat_axis=0, tiled=True)]
  transfers between devices with their start and end apart: 0 -> 1, of which waited for: 0 -> 0; matrix products, arithmetic and copies ran while one was open for 0% -> 1% of each run, Pallas kernels for 0% -> 3%
where the time goes in v3:
time: 260 us; the launch traced here: 259 us
  Pallas kernels  230 us (88%)
  other arithmetic  10.5 us (4%)
  starting transfers between devices  9.43 us (4%)
  local copies, waits for them, and re-layouts  6.87 us (3%)
    pallas_call x2, Pallas kernels, swap(): pl.pallas_call(functools.partial(swap_kernel, peers, groups, reach, len(s...  113 us
    pallas_call x1, Pallas kernels, fetch(): pl.pallas_call(functools.partial(fetch_kernel, peers, groups, reach), in_...  59.7 us
    pallas_call x1, Pallas kernels, attention(): pl.pallas_call(attention_kernel, grid_spec=pltpu.PrefetchScalarGridSpec(n...  33.1 us
    all_to_all x1, starting transfers between devices, on_device(): lax.all_to_all(copies, 'space', split_axis=0, concat_axis=0, tiled=True)  9.43 us
    pallas_call x1, Pallas kernels, finish(): pl.pallas_call(functools.partial(finish_kernel, cols // HEAD_DIM), grid=(...  8.73 us
    pallas_call x1, Pallas kernels, place(): pl.pallas_call(place_kernel, grid_spec=pltpu.PrefetchScalarGridSpec(num_s...  8.46 us
    pallas_call x1, Pallas kernels, project(): pl.pallas_call(functools.partial(project_kernel, cols // HEAD_DIM), grid=...  6.62 us
  transfers between devices with their start and end apart: 1, of which 0 were waited for; matrix products, arithmetic and copies ran while one was open for 1% of the time, Pallas kernels for 3%

profile of v3, /device:TPU:1, one launch (start us, length us, event | category | flops | bytes accessed | tf_op | source)
XLA Modules:
  0.0 259.4 jit_solution(11214085548563089514)
XLA Ops:
  0.6 1.3 broadcast_in_dim.18
  1.9 9.4 %all-to-all-start = ((s32[32,32,2]{1,2,0:T(2,128)}), s32[32,32,2]{1,2,0:T(2,128)S(1)}, u32[]{:S(2)}, u32[]{:S(2)}) async-start(s32[32,32,2]{1,2,0:T(2,128)} %broadcast_in_dim.18), calls=%async_computation | async-start | bytes 65536 | tf_op jit(solution)/shard_map/all_to_all | solution.py:563
  11.4 0.0 copy-start.5
  11.4 6.6 %shard_map.93 = (bf16[1024,1024]{1,0:T(8,128)(2,1)}, bf16[1024,256]{1,0:T(8,128)(2,1)}, bf16[8,4,128,128]{3,2,1,0:T(8,128)(2,1)S(1)}, f32[1024,1]{1,0:T(8,128)}, f32[1024,1]{1,0:T(8,128)}) custom-call(bf16[1024,1024]{1,0:T(8,128)(2,1)} %tokens_ref.3, bf16[3,1024,256]{2,1,0:T(8,128)(2,1)} %bitcast.30), custom_call_target="tpu_custom_call" | custom-call | tf_op jit(solution)/shard_map/pallas_call | solution.py:58
  18.0 1.2 reduce.1
  19.3 1.2 reduce.2
  20.5 0.0 all-to-all-done
  20.5 0.7 dynamic-slice_reduce_fusion
  21.2 0.1 reshape.41.wanted_ref
  21.4 0.6 fusion.8
  23.3 0.0 copy-done.5
  23.3 0.0 copy-start.1
  23.3 0.0 copy-start.2
  23.3 0.0 copy-start.4
  23.3 59.9 %conditional.2 = (bf16[4,1024,256]{2,1,0:T(8,128)(2,1)}, bf16[64,4,128,128]{3,2,1,0:T(8,128)(2,1)}) conditional(s32[]{:T(128)} %clamp.4, (s32[64]{0:T(128)S(1)}, bf16[8,4,128,128]{3,2,1,0:T(8,128)(2,1)S(1)}, bf16[1024,256]{1,0:T(8,128)(2,1)S(1)}) %tuple.76, (s32[64]{0:T(128)S(1)}, bf16[8,4,128,128]{3,2,1,0:T(8,128)(2,1)S(1)}, ...), branch_computations={%region_1.2_spmd, %region_2.3_spmd, %region_3.4_spmd} | conditional | bytes 16 | solution.py:572
  23.4 59.7 %branch_0_fun.2 = (bf16[32,2,4,128,128]{4,3,2,1,0:T(8,128)(2,1)}, bf16[4,1024,256]{2,1,0:T(8,128)(2,1)}) custom-call(s32[64]{0:T(128)S(1)} %get-tuple-element.58.wanted_ref, bf16[8,4,128,128]{3,2,1,0:T(8,128)(2,1)S(1)} %get-tuple-element.59.kv_ref, bf16[1024,256]{1,0:T(8,128)(2,1)S(1)} %get-tuple-element.60.cot_ref), custom_call_target="tpu_custom_call" | custom-call | tf_op jit(solution)/shard_map/cond/branch_0_fun/pallas_call | solution.py:189
  83.2 0.0 copy-done.1
  83.2 0.0 copy-done.2
  83.2 0.0 copy-done.4
  83.2 33.1 %shard_map.94 = (bf16[4,1024,256]{2,1,0:T(8,128)(2,1)}, f32[8,4,128,128]{3,2,1,0:T(8,128)S(1)}, bf16[64,4,128,128]{3,2,1,0:T(8,128)(2,1)}, bf16[1024,256]{1,0:T(8,128)(2,1)S(1)}, bf16[1024,512]{1,0:T(8,128)(2,1)S(1)}) custom-call(s32[8,9]{1,0:T(8,128)S(1)} %copy-done.4, bf16[1024,256]{1,0:T(8,128)(2,1)S(1)} %copy-done.2, ...), custom_call_target="tpu_custom_call" | custom-call | tf_op jit(solution)/shard_map/pallas_call | solution.py:415
  116.4 0.0 copy-start
  116.4 1.3 copy-done
  117.7 0.0 copy-start.3
  117.7 0.8 copy-done.3
  118.5 75.5 %conditional.3 = ((bf16[32,2,4,128,128]{4,3,2,1,0:T(8,128)(2,1)}, bf16[32,32,512]{2,1,0:T(8,128)(2,1)S(1)}, bf16[4,1024,256]{2,1,0:T(8,128)(2,1)})) conditional(s32[]{:T(128)} %clamp.4, (bf16[32,2,4,128,128]{4,3,2,1,0:T(8,128)(2,1)}, bf16[32,32,512]{2,1,0:T(8,128)(2,1)S(1)}, bf16[4,1024,256]{2,1,0:T(8,128)(2,1)}) %tuple.73, ...), branch_computations={%region_4.5_spmd, %region_5.6_spmd, %region_6.7_spmd} | conditional | bytes 8 | solution.py:589
  118.5 75.2 %branch_0_fun.3 = (bf16[32,2,4,128,128]{4,3,2,1,0:T(8,128)(2,1)}, bf16[32,32,512]{2,1,0:T(8,128)(2,1)S(1)}, bf16[4,1024,256]{2,1,0:T(8,128)(2,1)}) custom-call(bf16[32,2,4,128,128]{4,3,2,1,0:T(8,128)(2,1)} %get-tuple-element.73.refs_0_, bf16[32,32,512]{2,1,0:T(8,128)(2,1)S(1)} %get-tuple-element.74.refs_1_, bf16[4,1024,256]{2,1,0:T(8,128)(2,1)} %get-tuple-element.75.refs_2_), custom_call_target="tpu_custom_call" | custom-call | tf_op jit(solution)/shard_map/cond/branch_0_fun/pallas_call | solution.py:280
  194.0 0.2 convert_reduce_fusion.3
  194.1 0.6 slice_bitcast_fusion
  194.8 8.5 %shard_map.95.grad_kv_ref = bf16[8,4,128,128]{3,2,1,0:T(8,128)(2,1)} custom-call(s32[64]{0:T(128)S(1)} %reshape.41.wanted_ref, f32[8,4,128,128]{3,2,1,0:T(8,128)} %copy-done, bf16[64,4,128,128]{3,2,1,0:T(8,128)(2,1)} %bitcast.29), custom_call_target="tpu_custom_call" | custom-call | tf_op jit(solution)/shard_map/pallas_call | solution.py:476
  203.2 8.7 %shard_map.96 = (bf16[4,1024,256]{2,1,0:T(8,128)(2,1)}, f32[2,1024]{1,0:T(2,128)}, bf16[1024,512]{1,0:T(8,128)(2,1)}) custom-call(bf16[1024,1024]{1,0:T(8,128)(2,1)} %tokens_ref.3, bf16[1024,256]{1,0:T(8,128)(2,1)} %copy-done.3, bf16[8,4,128,128]{3,2,1,0:T(8,128)(2,1)} %shard_map.95.grad_kv_ref, bf16[3,1024,256]{2,1,0:T(8,128)(2,1)} %bitcast.31), custom_call_target="tpu_custom_call" | custom-call | tf_op jit(solution)/shard_map/pallas_call | solution.py:527
  212.0 1.3 broadcast_in_dim.20.refs_2_
  213.3 0.0 copy-start.7
  213.3 38.2 %shard_map.97 = (bf16[32,32,512]{2,1,0:T(8,128)(2,1)}, bf16[4,1024,256]{2,1,0:T(8,128)(2,1)}, f32[4,2,1024]{2,1,0:T(2,128)}) custom-call(bf16[32,32,512]{2,1,0:T(8,128)(2,1)} %bitcast.32, bf16[4,1024,256]{2,1,0:T(8,128)(2,1)} %get-tuple-element.121.refs_1_, f32[4,2,1024]{2,1,0:T(2,128)} %broadcast_in_dim.20.refs_2_), custom_call_target="tpu_custom_call" | custom-call | tf_op jit(solution)/shard_map/pallas_call | solution.py:280
  251.5 0.8 reduce_sum.51
  252.3 1.4 convert_reduce_fusion.2
  253.7 0.6 copy.18
  254.3 0.0 copy-done.7
  254.4 0.0 copy-start.6
  254.4 2.5 convert_reduce_fusion
  256.8 0.0 copy-done.6
  256.8 2.6 fusion.6
  (4 shorter events, 0.0 us)
Async XLA Ops:
  1.9 18.6 %all-to-all-start = ((s32[32,32,2]{1,2,0:T(2,128)}), s32[32,32,2]{1,2,0:T(2,128)S(1)}, u32[]{:S(2)}, u32[]{:S(2)}) async-start(s32[32,32,2]{1,2,0:T(2,128)} %broadcast_in_dim.18), calls=%async_computation | async-start | bytes 65536 | tf_op jit(solution)/shard_map/all_to_all | solution.py:563
  11.4 11.9 %copy-start.5 = (bf16[1024,256]{1,0:T(8,128)(2,1)S(1)}, bf16[1024,256]{1,0:T(8,128)(2,1)}, u32[]{:S(2)}) copy-start(bf16[1024,256]{1,0:T(8,128)(2,1)} %param.17) | copy-start | bytes 1572868
  23.3 59.9 %copy-start.1 = (bf16[256,1024]{1,0:T(8,128)(2,1)S(1)}, bf16[256,1024]{1,0:T(8,128)(2,1)}, u32[]{:S(2)}) copy-start(bf16[256,1024]{1,0:T(8,128)(2,1)} %w_out_ref.1) | copy-start | bytes 1572868
  23.3 59.9 %copy-start.2 = (bf16[1024,256]{1,0:T(8,128)(2,1)S(1)}, bf16[1024,256]{1,0:T(8,128)(2,1)}, u32[]{:S(2)}) copy-start(bf16[1024,256]{1,0:T(8,128)(2,1)} %get-tuple-element.107.q_ref) | copy-start | bytes 1572868
  23.3 59.9 %copy-start.4 = (s32[8,9]{1,0:T(8,128)S(1)}, s32[8,9]{1,0:T(8,128)}, u32[]{:S(2)}) copy-start(s32[8,9]{1,0:T(8,128)} %entries_ref.1) | copy-start | bytes 868
  116.4 1.3 copy-start
  117.7 0.8 copy-start.3
  213.3 41.1 %copy-start.7 = (bf16[4,1024,256]{2,1,0:T(8,128)(2,1)S(1)}, bf16[4,1024,256]{2,1,0:T(8,128)(2,1)}, u32[]{:S(2)}) copy-start(bf16[4,1024,256]{2,1,0:T(8,128)(2,1)} %get-tuple-element.148) | copy-start | bytes 6291460
  254.4 2.5 copy-start.6

commit v4 on v3

--- a/solution.py
+++ b/solution.py
@@ -35,12 +35,11 @@
     return slice(h * HEAD_DIM, (h + 1) * HEAD_DIM)
 
 
-def project_kernel(heads, tokens_ref, w_ref, normed_ref, q_ref, kv_ref, mean_ref, inverse_ref):
+def project_kernel(heads, tokens_ref, w_ref, normed_ref, q_ref, kv_ref, stats_ref):
     standard, mean, inverse = norm_rows(tokens_ref[...])
     normed = standard.astype(BF16)
     normed_ref[...] = normed
-    mean_ref[...] = mean
-    inverse_ref[...] = inverse
+    stats_ref[...] = jnp.concatenate([mean, inverse], 1).T
     q = dot(normed, w_ref[0], ((1,), (0,))).astype(BF16)
     q_ref[...] = (q.astype(F32) * HEAD_DIM ** (-0.5)).astype(BF16)
     k = dot(normed, w_ref[1], ((1,), (0,))).astype(BF16)
@@ -66,15 +65,13 @@
             pl.BlockSpec((step, width), lambda i: (i, 0)),
             pl.BlockSpec((step, cols), lambda i: (i, 0)),
             pl.BlockSpec(kv_block, lambda i: (i, 0, 0, 0)),
-            pl.BlockSpec((step, 1), lambda i: (i, 0)),
-            pl.BlockSpec((step, 1), lambda i: (i, 0)),
+            pl.BlockSpec((2, step), lambda i: (0, i)),
         ],
         out_shape=[
             jax.ShapeDtypeStruct((rows, width), BF16),
             jax.ShapeDtypeStruct((rows, cols), BF16),
             jax.ShapeDtypeStruct((rows // tile_rows,) + kv_block[1:], BF16),
-            jax.ShapeDtypeStruct((rows, 1), F32),
-            jax.ShapeDtypeStruct((rows, 1), F32),
+            jax.ShapeDtypeStruct((2, rows), F32),
         ],
         compiler_params=pltpu.CompilerParams(vmem_limit_bytes=VMEM_BYTES),
     )(tokens, w3)
@@ -92,6 +89,11 @@
 
 
 def greet(peers, groups):
+    signal_all(peers, groups)
+    pl.semaphore_wait(pltpu.get_barrier_semaphore(), peers + groups - 2)
+
+
+def signal_all(peers, groups):
     barrier = pltpu.get_barrier_semaphore()
     me, group = lax.axis_index("space"), lax.axis_index("head")
 
@@ -111,7 +113,6 @@
             device_id={"head": lax.rem(group + k, groups)},
             device_id_type=pl.DeviceIdType.MESH,
         )
-    pl.semaphore_wait(barrier, peers + groups - 2)
 
 
 def torus_order():
@@ -210,87 +211,79 @@
     )(wanted, kv, cot)
 
 
-def swap_kernel(peers, groups, reach, spaces, heads, slotted, *refs):
+def return_kernel(peers, groups, reach, wanted_ref, near_ref, far_ref, att_ref, grad_kv_ref, atts_ref, total, landed, sems, row_sems, own_sem):
     me, group = lax.axis_index("space"), lax.axis_index("head")
-    count = spaces + heads + slotted
-    sources, targets = refs[:count], refs[count : 2 * count]
-    sems, head_sems, own_sems = refs[2 * count :]
     greet(peers, groups)
-    owns = []
-    for i in range(slotted, count):
-        at = me if i < slotted + spaces else group
-        owns.append(pltpu.make_async_copy(sources[i].at[at], targets[i].at[at], own_sems.at[i]))
-        owns[-1].start()
-
-    def across(i, k):
+    own = pltpu.make_async_copy(att_ref.at[group], atts_ref.at[group], own_sem)
+    own.start()
+
+    def across(k):
         peer = lax.rem(group + k, groups)
+        return copy_to(att_ref.at[peer], atts_ref.at[group], row_sems, k, {"head": peer})
+
+    def along(c, r, peer):
         return copy_to(
-            sources[i].at[peer], targets[i].at[group], head_sems.at[i], k, {"head": peer}
-        )
-
-    def whole(i, r, peer):
-        return copy_to(sources[i].at[peer], targets[i].at[me], sems.at[i], r, {"space": peer})
-
-    def along(i, c, r, peer):
-        src, dst = sources[i].at[peer, c], targets[i].at[me, c]
-        return copy_to(src, dst, sems.at[i], c * peers + r, {"space": peer})
-
-    for i in range(slotted + spaces, count):
-        for k in range(1, groups):
-            across(i, k).start()
-    for r, step in enumerate(ORDER):
-        peer = torus_peer(me, step)
-        for i in range(slotted):
-            along(i, 0, r, peer).start()
-        for i in range(slotted, slotted + spaces):
-            whole(i, r, peer).start()
-    for i in range(slotted):
-        for low, high in second_ranges(peers, reach):
-
-            @pl.loop(low, high)
-            def _(r, i=i):
-                along(i, 1, r, lax.rem(me + r, peers)).start()
-
-    beside = lax.rem(me + 1, peers)
-
-    @pl.loop(0, len(ORDER))
-    def _(r):
-        for i in range(slotted):
-            along(i, 0, r, beside).wait()
-        for i in range(slotted, slotted + spaces):
-            whole(i, r, beside).wait()
-
-    for i in range(slotted):
-        for low, high in second_ranges(peers, reach):
-
-            @pl.loop(low, high)
-            def _(r, i=i):
-                along(i, 1, r, lax.rem(me + r, peers)).wait()
-
-    for i in range(slotted + spaces, count):
-        for k in range(1, groups):
-            across(i, k).wait()
-    for own in owns:
-        own.wait()
-
-
-def swap(slotted, spaces, heads, peers, groups, reach, number):
-    arrays = (*slotted, *spaces, *heads)
+            far_ref.at[peer, c], landed.at[r, c], sems, c * peers + r, {"space": peer}
+        )
+
+    for i, step in enumerate(ORDER):
+        along(0, i, torus_peer(me, step)).start()
+    for low, high in second_ranges(peers, reach):
+
+        @pl.loop(low, high)
+        def _(r):
+            along(1, r, lax.rem(me + r, peers)).start()
+
+    for k in range(1, groups):
+        across(k).start()
+    total[...] = near_ref[...]
+
+    def add(c, r, source):
+        tile = wanted_ref[source * SLOTS + c]
+        block = landed[r, c].astype(F32)
+
+        @pl.loop(0, total.shape[0])
+        def _(t):
+            total[t] += block * jnp.where(tile == t, 1.0, 0.0)
+
+    for i, step in enumerate(ORDER):
+        along(0, i, torus_peer(me, step)).wait()
+        add(0, i, torus_peer(me, ((4 - step[0]) % 4, (4 - step[1]) % 4, step[2])))
+    for low, high in second_ranges(peers, reach):
+
+        @pl.loop(low, high)
+        def _(r):
+            along(1, r, lax.rem(me + r, peers)).wait()
+            add(1, r, lax.rem(me + peers - r, peers))
+
+    grad_kv_ref[...] = total[...].astype(BF16)
+    for k in range(1, groups):
+        across(k).wait()
+    own.wait()
+
+
+def give_back(wanted, near, far, att, peers, groups, reach, number):
     whole = pl.BlockSpec(memory_space=pl.ANY)
+    vmem = pl.BlockSpec(memory_space=pltpu.VMEM)
     return pl.pallas_call(
-        functools.partial(
-            swap_kernel, peers, groups, reach, len(spaces), len(heads), len(slotted)
+        functools.partial(return_kernel, peers, groups, reach),
+        in_specs=[pl.BlockSpec(memory_space=pltpu.SMEM), vmem, whole, whole],
+        out_specs=[vmem, whole],
+        out_shape=[
+            jax.ShapeDtypeStruct(near.shape, BF16),
+            jax.ShapeDtypeStruct(att.shape, att.dtype),
+        ],
+        scratch_shapes=[
+            pltpu.VMEM(near.shape, F32),
+            pltpu.VMEM(far.shape, BF16),
+            pltpu.SemaphoreType.DMA((2, SLOTS * peers)),
+            pltpu.SemaphoreType.DMA((2, groups)),
+            pltpu.SemaphoreType.DMA,
+        ],
+        compiler_params=pltpu.CompilerParams(
+            collective_id=number, has_side_effects=True, vmem_limit_bytes=40 * 2**20
         ),
-        in_specs=[whole] * len(arrays),
-        out_specs=[whole] * len(arrays),
-        out_shape=[jax.ShapeDtypeStruct(a.shape, a.dtype) for a in arrays],
-        scratch_shapes=[
-            pltpu.SemaphoreType.DMA((len(arrays), 2, SLOTS * peers)),
-            pltpu.SemaphoreType.DMA((len(arrays), 2, groups)),
-            pltpu.SemaphoreType.DMA((len(arrays),)),
-        ],
-        compiler_params=pltpu.CompilerParams(collective_id=number, has_side_effects=True),
-    )(*arrays)
+    )(wanted, near, far, att)
 
 
 def attention_kernel(entries_ref, q_ref, cot_ref, w_out_ref, normed_ref, *refs):
@@ -449,103 +442,142 @@
     )(entries, q, cot, w_out, normed, *(([kv] * NEAR + [fetched] * (NEIGHBOURS - NEAR)) * AT_ONCE))
 
 
-def place_kernel(wanted_ref, near_ref, back_ref, grad_kv_ref, total):
-    step = pl.program_id(0)
-    count = back_ref.shape[0]
-
-    @pl.when(step == 0)
-    def _():
-        total[...] = near_ref[...]
-
-    for i in range(count):
-        tile = wanted_ref[step * count + i]
-
-        @pl.when(tile >= 0)
-        def _():
-            total[tile] += back_ref[i].astype(F32)
-
-    @pl.when(step == pl.num_programs(0) - 1)
-    def _():
-        grad_kv_ref[...] = total[...].astype(BF16)
-
-
-def place(wanted, near, back):
-    slots = back.shape[0]
-    step = 8
-    whole = lambda i, w: (0, 0, 0, 0)
-    return pl.pallas_call(
-        place_kernel,
-        grid_spec=pltpu.PrefetchScalarGridSpec(
-            num_scalar_prefetch=1,
-            grid=(slots // step,),
-            in_specs=[
-                pl.BlockSpec(near.shape, whole),
-                pl.BlockSpec((step,) + back.shape[1:], lambda i, w: (i, 0, 0, 0)),
-            ],
-            out_specs=pl.BlockSpec(near.shape, whole),
-            scratch_shapes=[pltpu.VMEM(near.shape, F32)],
-        ),
-        out_shape=jax.ShapeDtypeStruct(near.shape, BF16),
-        compiler_params=pltpu.CompilerParams(vmem_limit_bytes=VMEM_BYTES),
-    )(wanted, near, back)
-
-
-def finish_kernel(heads, tokens_ref, dq_ref, grad_kv_ref, w_ref, part_ref, sums_ref, grad_w_ref, total):
-    step = pl.program_id(0)
-
-    @pl.when(step == 0)
-    def _():
-        total[...] = jnp.zeros_like(total)
-
-    standard, _, _ = norm_rows(tokens_ref[...])
-    pairs = [
-        jnp.concatenate([grad_kv_ref[t, h].T for t in range(grad_kv_ref.shape[0])], 0)
-        for h in range(heads)
+def finish_kernel(peers, groups, tokens_ref, dq_ref, grad_kv_ref, w_ref, early_ref, earlies_ref, lates_ref, parts_ref, sums_ref, grads, normed, part, late, sums, stats, sems, row_sems, own_sems):
+    me, group = lax.axis_index("space"), lax.axis_index("head")
+    signal_all(peers, groups)
+    rows, width = tokens_ref.shape
+    cols = dq_ref.shape[1]
+    share = width // groups
+    tiles, heads = grad_kv_ref.shape[:2]
+    span = rows // tiles
+    step = 256
+
+    @pl.loop(0, rows // step)
+    def _(i):
+        at = pl.ds(pl.multiple_of(i * step, step), step)
+        standard, mean, inverse = norm_rows(tokens_ref[at, :])
+        normed[at, :] = standard.astype(BF16)
+        stats[0, at, :] = jnp.broadcast_to(mean, (step, 128))
+        stats[1, at, :] = jnp.broadcast_to(inverse, (step, 128))
+        grads[at, :cols] = dq_ref[at, :]
+
+    for t in range(tiles):
+        pairs = [grad_kv_ref[t, h].T for h in range(heads)]
+        at = slice(t * span, (t + 1) * span)
+        grads[at, cols : 2 * cols] = jnp.concatenate([p[:, :HEAD_DIM] for p in pairs], 1)
+        grads[at, 2 * cols :] = jnp.concatenate([p[:, HEAD_DIM:] for p in pairs], 1)
+
+    def chunk(k):
+        at_cols = pl.ds(pl.multiple_of(lax.rem(group + k, groups) * share, share), share)
+
+        @pl.loop(0, rows // step)
+        def _(i):
+            at = pl.ds(pl.multiple_of(i * step, step), step)
+            piece = dot(grads[at, :cols], w_ref[0, at_cols, :], ((1,), (1,)))
+            for n in (1, 2):
+                lanes = slice(n * cols, (n + 1) * cols)
+                piece += dot(grads[at, lanes], w_ref[n, at_cols, :], ((1,), (1,)))
+            part[k, at, :] = piece.astype(BF16)
+            values = tokens_ref[at, at_cols].astype(F32)
+            standard = (values - stats[0, at, :1]) * stats[1, at, :1]
+            found = [
+                jnp.sum(piece, 1, keepdims=True),
+                jnp.sum(piece * standard, 1, keepdims=True),
+            ]
+            found = jnp.concatenate(found, 1).T
+            if k == 0:
+                sums[:, at] = found
+            else:
+                sums[:, at] += found
+
+    def across(k):
+        return copy_to(
+            part.at[k], parts_ref.at[group], row_sems, k, {"head": lax.rem(group + k, groups)}
+        )
+
+    def across_sums(k):
+        return copy_to(
+            sums, sums_ref.at[group], row_sems, groups + k, {"head": lax.rem(group + k, groups)}
+        )
+
+    def along(kind, r, peer):
+        source, target = ((early_ref, earlies_ref), (late, lates_ref))[kind]
+        return copy_to(
+            source.at[peer], target.at[me], sems, kind * peers + r, {"space": peer}
+        )
+
+    owns = [
+        pltpu.make_async_copy(early_ref.at[me], earlies_ref.at[me], own_sems.at[0]),
+        pltpu.make_async_copy(late.at[me], lates_ref.at[me], own_sems.at[1]),
+        pltpu.make_async_copy(part.at[0], parts_ref.at[group], own_sems.at[2]),
+        pltpu.make_async_copy(sums, sums_ref.at[group], own_sems.at[3]),
     ]
-    dk = jnp.concatenate([p[:, :HEAD_DIM] for p in pairs], 1)
-    dv = jnp.concatenate([p[:, HEAD_DIM:] for p in pairs], 1)
-    total[...] += dot(standard.astype(BF16), jnp.concatenate([dk, dv], 1), ((0,), (0,)))
-    part = dot(dq_ref[...], w_ref[0], ((1,), (1,)))
-    part += dot(dk, w_ref[1], ((1,), (1,)))
-    part += dot(dv, w_ref[2], ((1,), (1,)))
-    sums = [jnp.sum(part, 1, keepdims=True), jnp.sum(part * standard, 1, keepdims=True)]
-    sums_ref[...] = jnp.concatenate(sums, 1).T
-    share = part_ref.shape[2]
-    for g in range(part_ref.shape[0]):
-        part_ref[g] = part[:, g * share : (g + 1) * share].astype(BF16)
-
-    @pl.when(step == pl.num_programs(0) - 1)
-    def _():
-        grad_w_ref[...] = total[...].astype(BF16)
-
-
-def finish(tokens, dq, grad_kv, w3, groups):
+    owns[0].start()
+    chunk(0)
+    owns[2].start()
+    pl.semaphore_wait(pltpu.get_barrier_semaphore(), peers + groups - 2)
+    for r, torus in enumerate(ORDER):
+        along(0, r, torus_peer(me, torus)).start()
+    for k in (2, 1, 3):
+        chunk(k)
+        across(k).start()
+    owns[3].start()
+    for k in range(1, groups):
+        across_sums(k).start()
+
+    piece = width // 4
+    for i in range(4):
+        made = dot(normed[:, i * piece : (i + 1) * piece], grads[:, cols:], ((0,), (0,)))
+        late[i * peers // 4 : (i + 1) * peers // 4] = made.astype(BF16).reshape(
+            peers // 4, width // peers, 2 * cols
+        )
+    owns[1].start()
+    for r, torus in enumerate(ORDER):
+        along(1, r, torus_peer(me, torus)).start()
+
+    @pl.loop(0, len(ORDER))
+    def _(r):
+        along(0, r, lax.rem(me + 1, peers)).wait()
+        along(1, r, lax.rem(me + 1, peers)).wait()
+
+    for k in range(1, groups):
+        across(k).wait()
+        across_sums(k).wait()
+    for own in owns:
+        own.wait()
+
+
+def finish(tokens, dq, grad_kv, w3, early, peers, groups, number):
     rows, width = tokens.shape
     cols = dq.shape[1]
-    step = 256
-    row2 = lambda i: (i, 0)
+    whole = pl.BlockSpec(memory_space=pl.ANY)
+    vmem = pl.BlockSpec(memory_space=pltpu.VMEM)
+    part = (groups, rows, width // groups)
     return pl.pallas_call(
-        functools.partial(finish_kernel, cols // HEAD_DIM),
-        grid=(rows // step,),
-        in_specs=[
-            pl.BlockSpec((step, width), row2),
-            pl.BlockSpec((step, cols), row2),
-            pl.BlockSpec((step // grad_kv.shape[2],) + grad_kv.shape[1:], lambda i: (i, 0, 0, 0)),
-            pl.BlockSpec((3, width, cols), lambda i: (0, 0, 0)),
-        ],
-        out_specs=[
-            pl.BlockSpec((groups, step, width // groups), lambda i: (0, i, 0)),
-            pl.BlockSpec((2, step), lambda i: (0, i)),
-            pl.BlockSpec((width, 2 * cols), lambda i: (0, 0)),
-        ],
+        functools.partial(finish_kernel, peers, groups),
+        in_specs=[vmem] * 4 + [whole],
+        out_specs=[whole] * 4,
         out_shape=[
-            jax.ShapeDtypeStruct((groups, rows, width // groups), BF16),
-            jax.ShapeDtypeStruct((2, rows), F32),
-            jax.ShapeDtypeStruct((width, 2 * cols), BF16),
-        ],
-        scratch_shapes=[pltpu.VMEM((width, 2 * cols), F32)],
-        compiler_params=pltpu.CompilerParams(vmem_limit_bytes=VMEM_BYTES),
-    )(tokens, dq, grad_kv, w3)
+            jax.ShapeDtypeStruct(early.shape, BF16),
+            jax.ShapeDtypeStruct(early.shape, BF16),
+            jax.ShapeDtypeStruct(part, BF16),
+            jax.ShapeDtypeStruct((groups, 2, rows), F32),
+        ],
+        scratch_shapes=[
+            pltpu.VMEM((rows, 3 * cols), BF16),
+            pltpu.VMEM((rows, width), BF16),
+            pltpu.VMEM(part, BF16),
+            pltpu.VMEM(early.shape, BF16),
+            pltpu.VMEM((2, rows), F32),
+            pltpu.VMEM((2, rows, 128), F32),
+            pltpu.SemaphoreType.DMA((2, 2 * peers)),
+            pltpu.SemaphoreType.DMA((2, 2 * groups)),
+            pltpu.SemaphoreType.DMA((4,)),
+        ],
+        compiler_params=pltpu.CompilerParams(
+            collective_id=number, has_side_effects=True, vmem_limit_bytes=40 * 2**20
+        ),
+    )(tokens, dq, grad_kv, w3, early)
 
 
 def on_device(tokens, w_qkv, w_out, neighbours, requests, cotangent):
@@ -568,7 +600,7 @@
     level = (reach > REACHES[0]).astype(jnp.int32) + (reach > REACHES[1]).astype(jnp.int32)
     reaches = (*REACHES, peers)
 
-    normed, q, kv, mean, inverse = project(tokens, w3, rows)
+    normed, q, kv, stats = project(tokens, w3, rows)
     fetched, cots = lax.switch(
         level,
         [
@@ -583,27 +615,27 @@
         neighbours, q, cots, w_out, normed, kv, fetched.reshape((-1,) + kv.shape[1:])
     )
 
-    def give_back(far, early, attended, reach, number):
-        return swap((far,), (early,), (attended,), peers, groups, reach, number)
-
-    back, early, attended = lax.switch(
+    grad_kv, attended = lax.switch(
         level,
         [
-            functools.partial(give_back, reach=r, number=n + len(reaches))
+            functools.partial(
+                give_back, peers=peers, groups=groups, reach=r, number=n + len(reaches)
+            )
             for n, r in enumerate(reaches)
         ],
+        wanted,
+        near,
         far.reshape(fetched.shape),
-        early.reshape(peers, width // peers, 2 * cols),
         attended,
     )
-    grad_kv = place(wanted, near, back.reshape(far.shape))
-    part, sums, late = finish(tokens, dq, grad_kv, w3, groups)
-    sums = jnp.broadcast_to(sums, (groups,) + sums.shape)
-    late = late.reshape(peers, width // peers, 2 * cols)
-    late, part, sums = swap((), (late,), (part, sums), peers, groups, peers, 2 * len(reaches))
+    early = early.reshape(peers, width // peers, 2 * cols)
+    early, late, part, sums = finish(
+        tokens, dq, grad_kv, w3, early, peers, groups, 2 * len(reaches)
+    )
 
     own_tokens = lax.dynamic_slice_in_dim(tokens, column, share, 1).astype(F32)
     layer_out = (own_tokens + jnp.sum(attended.astype(F32), 0)).astype(BF16)
+    mean, inverse = stats[0][:, None], stats[1][:, None]
     own_standard = (own_tokens - mean) * inverse
     own_part = jnp.sum(part.astype(F32), 0)
     means = (jnp.sum(sums, 0) / width)[:, :, None]

time: 260 us -> 231 us (0.89)
  Pallas kernels: 230 us -> 199 us
  local copies, waits for them, and re-layouts: 6.87 us -> 13.2 us
  other arithmetic: 10.5 us -> 5.62 us
    pallas_call x4 -> x2, Pallas kernels: 131 us -> 102 us  [the longest x1 64.9 us: give_back(): pl.pallas_call(functools.partial(return_kernel, peers, groups, reach), in...]
    unnamed x16 -> x30, local copies, waits for them, and re-layouts: 2.15 us -> 5.8 us
    cond x0 -> x2, local copies, waits for them, and re-layouts: none -> 3.22 us
  transfers between devices with their start and end apart: 1 -> 1, of which waited for: 0 -> 1; matrix products, arithmetic and copies ran while one was open for 1% -> 0% of each run, Pallas kernels for 3% -> 3%
where the time goes in v4:
time: 231 us; the launch traced here: 230 us
  Pallas kernels  199 us (86%)
  local copies, waits for them, and re-layouts  13.2 us (6%)
  starting transfers between devices  9.43 us (4%)
  other arithmetic  5.62 us (2%)
    pallas_call x1, Pallas kernels, give_back(): pl.pallas_call(functools.partial(return_kernel, peers, groups, reach), in...  64.9 us
    pallas_call x1, Pallas kernels, fetch(): pl.pallas_call(functools.partial(fetch_kernel, peers, groups, reach), in_...  59.3 us
    pallas_call x1, Pallas kernels, finish(): pl.pallas_call(functools.partial(finish_kernel, peers, groups), in_specs=...  37.3 us
    pallas_call x1, Pallas kernels, attention(): pl.pallas_call(attention_kernel, grid_spec=pltpu.PrefetchScalarGridSpec(n...  31.3 us
    all_to_all x1, starting transfers between devices, on_device(): lax.all_to_all(copies, 'space', split_axis=0, concat_axis=0, tiled=True)  9.43 us
    pallas_call x1, Pallas kernels, project(): pl.pallas_call(functools.partial(project_kernel, cols // HEAD_DIM), grid=...  6.11 us
    unnamed x30, local copies, waits for them, and re-layouts  5.8 us
  transfers between devices with their start and end apart: 1, of which 1 were waited for; matrix products, arithmetic and copies ran while one was open for 0% of the time, Pallas kernels for 3%

profile of v4, /device:TPU:1, one launch (start us, length us, event | category | flops | bytes accessed | tf_op | source)
XLA Modules:
  0.0 230.2 jit_solution(4053738123825833195)
XLA Ops:
  0.6 0.0 copy-start.11
  0.6 1.4 broadcast_in_dim.15
  2.0 9.4 %all-to-all-start = ((s32[32,32,2]{1,2,0:T(2,128)}), s32[32,32,2]{1,2,0:T(2,128)S(1)}, u32[]{:S(2)}, u32[]{:S(2)}) async-start(s32[32,32,2]{1,2,0:T(2,128)} %broadcast_in_dim.15), calls=%async_computation | async-start | bytes 65536 | tf_op jit(solution)/shard_map/all_to_all | solution.py:595
  11.4 6.1 %shard_map.93 = (bf16[1024,1024]{1,0:T(8,128)(2,1)}, bf16[1024,256]{1,0:T(8,128)(2,1)}, bf16[8,4,128,128]{3,2,1,0:T(8,128)(2,1)S(1)}, f32[2,1024]{1,0:T(2,128)}) custom-call(bf16[1024,1024]{1,0:T(8,128)(2,1)} %tokens_ref.3, bf16[3,1024,256]{2,1,0:T(8,128)(2,1)} %bitcast.22), custom_call_target="tpu_custom_call" | custom-call | tf_op jit(solution)/shard_map/pallas_call | solution.py:57
  17.6 0.8 fusion.9
  18.3 0.4 all-to-all-done
  18.7 0.7 dynamic-slice_reduce_fusion
  19.4 0.1 reshape.44
  19.5 0.6 fusion.8
  21.5 0.0 copy-done.11
  21.5 0.0 copy-start.5
  21.5 0.0 copy-start.6
  21.5 0.0 copy-start.9
  21.5 59.5 %conditional.2 = (bf16[4,1024,256]{2,1,0:T(8,128)(2,1)}, bf16[64,4,128,128]{3,2,1,0:T(8,128)(2,1)}) conditional(s32[]{:T(128)} %clamp.4, (s32[64]{0:T(128)S(1)}, bf16[8,4,128,128]{3,2,1,0:T(8,128)(2,1)S(1)}, bf16[1024,256]{1,0:T(8,128)(2,1)S(1)}) %tuple.54, (s32[64]{0:T(128)S(1)}, bf16[8,4,128,128]{3,2,1,0:T(8,128)(2,1)S(1)}, ...), branch_computations={%region_1.2_spmd, %region_2.3_spmd, %region_3.4_spmd} | conditional | bytes 16 | solution.py:604
  21.5 59.3 %branch_0_fun.2 = (bf16[32,2,4,128,128]{4,3,2,1,0:T(8,128)(2,1)}, bf16[4,1024,256]{2,1,0:T(8,128)(2,1)}) custom-call(s32[64]{0:T(128)S(1)} %get-tuple-element.59.wanted_ref, bf16[8,4,128,128]{3,2,1,0:T(8,128)(2,1)S(1)} %get-tuple-element.60.kv_ref, bf16[1024,256]{1,0:T(8,128)(2,1)S(1)} %get-tuple-element.61.cot_ref), custom_call_target="tpu_custom_call" | custom-call | tf_op jit(solution)/shard_map/cond/branch_0_fun/pallas_call | solution.py:190
  81.0 0.0 copy-done.5
  81.0 0.0 copy-done.6
  81.0 0.0 copy-done.9
  81.0 31.3 %shard_map.94 = (bf16[4,1024,256]{2,1,0:T(8,128)(2,1)}, f32[8,4,128,128]{3,2,1,0:T(8,128)}, bf16[64,4,128,128]{3,2,1,0:T(8,128)(2,1)S(1)}, bf16[1024,256]{1,0:T(8,128)(2,1)S(1)}, bf16[1024,512]{1,0:T(8,128)(2,1)S(1)}) custom-call(s32[8,9]{1,0:T(8,128)S(1)} %copy-done.9, bf16[1024,256]{1,0:T(8,128)(2,1)S(1)} %copy-done.6, ...), custom_call_target="tpu_custom_call" | custom-call | tf_op jit(solution)/shard_map/pallas_call | solution.py:408
  112.3 0.0 copy-start.3
  112.4 0.0 copy-start.7
  112.4 0.0 copy-start
  112.4 1.0 copy-done.3
  113.4 0.1 copy-done.7
  113.5 68.7 %conditional.3 = (bf16[8,4,128,128]{3,2,1,0:T(8,128)(2,1)}, f32[1024,256]{1,0:T(8,128)S(1)}) conditional(s32[]{:T(128)} %clamp.4, (bf16[64,4,128,128]{3,2,1,0:T(8,128)(2,1)S(1)}, s32[64]{0:T(128)S(1)}, f32[8,4,128,128]{3,2,1,0:T(8,128)}, bf16[4,1024,256]{2,1,0:T(8,128)(2,1)}) %tuple.39, (bf16[64,4,128,128]{3,2,1,0:T(8,128)(2,1)S(1)}, ...), branch_computations={%region_4.6_spmd, %region_6.8_spmd, %region_8.10_spmd} | conditional | flops 1835008 | bytes 36700204 | solution.py:618
  113.5 0.0 copy-start.10
  113.5 3.2 %copy-done.10 = bf16[64,4,128,128]{3,2,1,0:T(8,128)(2,1)} copy-done((bf16[64,4,128,128]{3,2,1,0:T(8,128)(2,1)}, bf16[64,4,128,128]{3,2,1,0:T(8,128)(2,1)S(1)}, u32[]{:S(2)}) %copy-start.10) | copy-done | bytes 8388632 | tf_op jit(solution)/shard_map/cond
  116.7 64.9 %branch_0_fun.3 = (bf16[8,4,128,128]{3,2,1,0:T(8,128)(2,1)}, bf16[4,1024,256]{2,1,0:T(8,128)(2,1)S(1)}) custom-call(s32[64]{0:T(128)S(1)} %get-tuple-element.74.wanted_ref, f32[8,4,128,128]{3,2,1,0:T(8,128)} %get-tuple-element.75.near_ref, bf16[32,2,4,128,128]{4,3,2,1,0:T(8,128)(2,1)} %bitcast.28, bf16[4,1024,256]{2,1,0:T(8,128)(2,1)} %get-tuple-element.77.att_ref), custom_call_target="tpu_custom_call" | custom-call | tf_op jit(solution)/shard_map/cond/branch_0_fun/pallas_call | solution.py:268
  181.6 0.3 convert_reduce_fusion
  182.2 0.0 copy-start.14
  182.2 1.0 copy-done.14
  183.2 0.0 copy-done
  183.2 0.0 copy-start.1
  183.2 1.4 copy-done.1
  184.6 0.0 copy-start.4
  184.6 1.2 copy-done.4
  185.8 0.0 copy-start.8
  185.8 1.0 copy-done.8
  186.8 37.3 %shard_map.95 = (bf16[32,32,512]{2,1,0:T(8,128)(2,1)S(1)}, bf16[32,32,512]{2,1,0:T(8,128)(2,1)S(1)}, bf16[4,1024,256]{2,1,0:T(8,128)(2,1)S(1)}, f32[4,2,1024]{2,1,0:T(2,128)S(1)}) custom-call(bf16[1024,1024]{1,0:T(8,128)(2,1)S(1)} %copy-done, bf16[1024,256]{1,0:T(8,128)(2,1)S(1)} %copy-done.8, bf16[8,4,128,128]{3,2,1,0:T(8,128)(2,1)} %get-tuple-element.124.grad_kv_ref, ...), custom_call_target="tpu_custom_call" | custom-call | tf_op jit(solution)/shard_map/pallas_call | solution.py:556
  224.2 0.0 copy-start.2
  224.2 1.3 convert_reduce_fusion.3
  225.5 0.0 copy-done.2
  225.5 0.0 copy-start.12
  225.5 0.0 copy-start.13
  225.5 0.0 copy-start.15
  225.6 1.7 convert_reduce_fusion.4
  227.3 0.6 slice_bitcast_fusion
  227.9 0.6 copy.18
  228.5 0.0 copy-done.12
  228.5 0.0 copy-done.13
  228.5 0.0 copy-done.15
  228.5 1.6 fusion.6
  (5 shorter events, 0.1 us)
Async XLA Ops:
  0.6 20.8 %copy-start.11 = (bf16[1024,256]{1,0:T(8,128)(2,1)S(1)}, bf16[1024,256]{1,0:T(8,128)(2,1)}, u32[]{:S(2)}) copy-start(bf16[1024,256]{1,0:T(8,128)(2,1)} %param.17) | copy-start | bytes 1572868
  2.0 16.7 %all-to-all-start = ((s32[32,32,2]{1,2,0:T(2,128)}), s32[32,32,2]{1,2,0:T(2,128)S(1)}, u32[]{:S(2)}, u32[]{:S(2)}) async-start(s32[32,32,2]{1,2,0:T(2,128)} %broadcast_in_dim.15), calls=%async_computation | async-start | bytes 65536 | tf_op jit(solution)/shard_map/all_to_all | solution.py:595
  21.5 59.5 %copy-start.5 = (bf16[256,1024]{1,0:T(8,128)(2,1)S(1)}, bf16[256,1024]{1,0:T(8,128)(2,1)}, u32[]{:S(2)}) copy-start(bf16[256,1024]{1,0:T(8,128)(2,1)} %w_out_ref.1) | copy-start | bytes 1572868
  21.5 59.5 %copy-start.6 = (bf16[1024,256]{1,0:T(8,128)(2,1)S(1)}, bf16[1024,256]{1,0:T(8,128)(2,1)}, u32[]{:S(2)}) copy-start(bf16[1024,256]{1,0:T(8,128)(2,1)} %get-tuple-element.113.q_ref) | copy-start | bytes 1572868
  21.5 59.5 %copy-start.9 = (s32[8,9]{1,0:T(8,128)S(1)}, s32[8,9]{1,0:T(8,128)}, u32[]{:S(2)}) copy-start(s32[8,9]{1,0:T(8,128)} %entries_ref.1) | copy-start | bytes 868
  112.3 1.1 copy-start.3
  112.4 1.1 copy-start.7
  112.4 70.8 %copy-start = (bf16[1024,1024]{1,0:T(8,128)(2,1)S(1)}, bf16[1024,1024]{1,0:T(8,128)(2,1)}, u32[]{:S(2)}) copy-start(bf16[1024,1024]{1,0:T(8,128)(2,1)} %tokens_ref.3) | copy-start | bytes 6291460
  113.5 3.2 %copy-start.10 = (bf16[64,4,128,128]{3,2,1,0:T(8,128)(2,1)}, bf16[64,4,128,128]{3,2,1,0:T(8,128)(2,1)S(1)}, u32[]{:S(2)}) copy-start(bf16[64,4,128,128]{3,2,1,0:T(8,128)(2,1)S(1)} %get-tuple-element.76) | copy-start | bytes 25165828 | tf_op jit(solution)/shard_map/cond
  182.2 1.0 copy-start.14
  183.2 1.4 copy-start.1
  184.6 1.2 copy-start.4
  185.8 1.0 copy-start.8
  224.2 1.3 copy-start.2
  225.5 3.0 %copy-start.12 = (bf16[1024,256]{1,0:T(8,128)(2,1)S(1)}, bf16[1024,256]{1,0:T(8,128)(2,1)}, u32[]{:S(2)}) copy-start(bf16[1024,256]{1,0:T(8,128)(2,1)} %param.17) | copy-start | bytes 1572868
  225.5 3.0 %copy-start.13 = (f32[1024,256]{1,0:T(8,128)S(1)}, f32[1024,256]{1,0:T(8,128)}, u32[]{:S(2)}) copy-start(f32[1024,256]{1,0:T(8,128)} %convert_reduce_fusion.3) | copy-start | bytes 3145732
  225.5 3.0 %copy-start.15 = (f32[1024,256]{1,0:T(8,128)S(1)}, f32[1024,256]{1,0:T(8,128)}, u32[]{:S(2)}) copy-start(f32[1024,256]{1,0:T(8,128)} %copy-done.14) | copy-start | bytes 3145732

commit v5 on v4

--- a/solution.py
+++ b/solution.py
@@ -35,7 +35,20 @@
     return slice(h * HEAD_DIM, (h + 1) * HEAD_DIM)
 
 
-def project_kernel(heads, tokens_ref, w_ref, normed_ref, q_ref, kv_ref, stats_ref):
+def project_kernel(peers, groups, tokens_ref, w_ref, requests_ref, normed_ref, q_ref, kv_ref, stats_ref, table_ref, sems, own_sem):
+    me = lax.axis_index("space")
+    step = pl.program_id(0)
+    heads = kv_ref.shape[1]
+    own = pltpu.make_async_copy(requests_ref, table_ref.at[me], own_sem)
+
+    def along(r, peer):
+        return copy_to(requests_ref, table_ref.at[me], sems, r, {"space": peer})
+
+    @pl.when(step == 0)
+    def _():
+        own.start()
+        signal_all(peers, groups)
+
     standard, mean, inverse = norm_rows(tokens_ref[...])
     normed = standard.astype(BF16)
     normed_ref[...] = normed
@@ -48,33 +61,55 @@
         pair = jnp.concatenate([k[:, head_cut(h)], v[:, head_cut(h)]], 1)
         kv_ref[:, h] = pair.reshape(kv_ref.shape[0], kv_ref.shape[2], 2 * HEAD_DIM)
 
-
-def project(tokens, w3, tile_rows):
+    @pl.when(step == 2)
+    def _():
+        pl.semaphore_wait(pltpu.get_barrier_semaphore(), peers + groups - 2)
+
+        @pl.loop(1, peers)
+        def _(r):
+            along(r, lax.rem(me + r, peers)).start()
+
+    @pl.when(step == pl.num_programs(0) - 1)
+    def _():
+        @pl.loop(1, peers)
+        def _(r):
+            along(r, lax.rem(me + r, peers)).wait()
+
+        own.wait()
+
+
+def project(tokens, w3, requests, tile_rows, peers, groups, number):
     rows, width = tokens.shape
     cols = w3.shape[2]
     step = 256
     kv_block = (step // tile_rows, cols // HEAD_DIM, tile_rows, 2 * HEAD_DIM)
     return pl.pallas_call(
-        functools.partial(project_kernel, cols // HEAD_DIM),
+        functools.partial(project_kernel, peers, groups),
         grid=(rows // step,),
         in_specs=[
             pl.BlockSpec((step, width), lambda i: (i, 0)),
             pl.BlockSpec((3, width, cols), lambda i: (0, 0, 0)),
+            pl.BlockSpec(memory_space=pl.ANY),
         ],
         out_specs=[
             pl.BlockSpec((step, width), lambda i: (i, 0)),
             pl.BlockSpec((step, cols), lambda i: (i, 0)),
             pl.BlockSpec(kv_block, lambda i: (i, 0, 0, 0)),
             pl.BlockSpec((2, step), lambda i: (0, i)),
+            pl.BlockSpec(memory_space=pl.ANY),
         ],
         out_shape=[
             jax.ShapeDtypeStruct((rows, width), BF16),
             jax.ShapeDtypeStruct((rows, cols), BF16),
             jax.ShapeDtypeStruct((rows // tile_rows,) + kv_block[1:], BF16),
             jax.ShapeDtypeStruct((2, rows), F32),
-        ],
-        compiler_params=pltpu.CompilerParams(vmem_limit_bytes=VMEM_BYTES),
-    )(tokens, w3)
+            jax.ShapeDtypeStruct((peers,) + requests.shape, requests.dtype),
+        ],
+        scratch_shapes=[pltpu.SemaphoreType.DMA((2, peers)), pltpu.SemaphoreType.DMA],
+        compiler_params=pltpu.CompilerParams(
+            collective_id=number, has_side_effects=True, vmem_limit_bytes=VMEM_BYTES
+        ),
+    )(tokens, w3, requests)
 
 
 def copy_to(src, dst, sems, index, device):
@@ -159,14 +194,14 @@
         across(k).start()
     for i, step in enumerate(ORDER):
         peer = torus_peer(me, step)
-        staged[i, 0] = kv_ref[jnp.maximum(wanted_ref[peer * SLOTS], 0)]
+        staged[i, 0] = kv_ref[jnp.maximum(wanted_ref[peer], 0)]
         along(0, i, peer).start()
     for low, high in second_ranges(peers, reach):
 
         @pl.loop(low, high)
         def _(r):
             peer = lax.rem(me + r, peers)
-            staged[r, 1] = kv_ref[jnp.maximum(wanted_ref[peer * SLOTS + 1], 0)]
+            staged[r, 1] = kv_ref[jnp.maximum(wanted_ref[peers + peer], 0)]
             along(1, r, peer).start()
 
     @pl.loop(0, len(ORDER))
@@ -239,7 +274,7 @@
     total[...] = near_ref[...]
 
     def add(c, r, source):
-        tile = wanted_ref[source * SLOTS + c]
+        tile = wanted_ref[c * peers + source]
         block = landed[r, c].astype(F32)
 
         @pl.loop(0, total.shape[0])
@@ -281,7 +316,7 @@
             pltpu.SemaphoreType.DMA,
         ],
         compiler_params=pltpu.CompilerParams(
-            collective_id=number, has_side_effects=True, vmem_limit_bytes=40 * 2**20
+            collective_id=number, has_side_effects=True, vmem_limit_bytes=VMEM_BYTES
         ),
     )(wanted, near, far, att)
 
@@ -575,7 +610,7 @@
             pltpu.SemaphoreType.DMA((4,)),
         ],
         compiler_params=pltpu.CompilerParams(
-            collective_id=number, has_side_effects=True, vmem_limit_bytes=40 * 2**20
+            collective_id=number, has_side_effects=True, vmem_limit_bytes=VMEM_BYTES
         ),
     )(tokens, dq, grad_kv, w3, early)
 
@@ -591,16 +626,16 @@
     column = lax.axis_index("head") * share
     w3 = jnp.transpose(w_qkv, (1, 0, 2))
 
-    copies = jnp.broadcast_to(requests, (peers,) + requests.shape[1:])
-    table = lax.all_to_all(copies, "space", split_axis=0, concat_axis=0, tiled=True)
-    wanted = lax.dynamic_index_in_dim(table, me, 1, keepdims=False).reshape(-1)
+    normed, q, kv, stats, table = project(
+        tokens, w3, requests[0].T, rows, peers, groups, 2 * len(REACHES) + 3
+    )
+    wanted = lax.dynamic_index_in_dim(table, me, 2, keepdims=False).T.reshape(-1)
     apart = jnp.abs(jnp.arange(peers)[:, None] - jnp.arange(peers)[None, :])
     apart = jnp.minimum(apart, peers - apart)
-    reach = jnp.max(jnp.where(jnp.any(table[:, :, 1:] >= 0, axis=2), apart, 0))
+    reach = jnp.max(jnp.where(jnp.any(table[:, 1:] >= 0, axis=1), apart, 0))
     level = (reach > REACHES[0]).astype(jnp.int32) + (reach > REACHES[1]).astype(jnp.int32)
     reaches = (*REACHES, peers)
 
-    normed, q, kv, stats = project(tokens, w3, rows)
     fetched, cots = lax.switch(
         level,
         [

time: 231 us -> 224 us (0.970)
  starting transfers between devices: 9.43 us -> 0 us
  Pallas kernels: 199 us -> 208 us
  local copies, waits for them, and re-layouts: 13.2 us -> 4.88 us
  other arithmetic: 5.62 us -> 8.47 us
    pallas_call x1, Pallas kernels: 6.11 us -> 16.4 us  [project(): pl.pallas_call(functools.partial(project_kernel, peers, groups), grid=(ro...]
    all_to_all x1 -> x0, starting transfers between devices: 9.43 us -> none  [on_device(): lax.all_to_all(copies, 'space', split_axis=0, concat_axis=0, tiled=True)]
    unnamed x30 -> x18, local copies, waits for them, and re-layouts: 5.8 us -> 1.79 us
    cond x2 -> x0, local copies, waits for them, and re-layouts: 3.22 us -> none
    pallas_call x1, Pallas kernels: 31.3 us -> 33.8 us  [attention(): pl.pallas_call(attention_kernel, grid_spec=pltpu.PrefetchScalarGridSpec(n...]
  transfers between devices with their start and end apart: 1 -> 0, of which waited for: 1 -> 0; matrix products, arithmetic and copies ran while one was open for 0% -> 0% of each run, Pallas kernels for 3% -> 0%
where the time goes in v5:
time: 224 us
  Pallas kernels  208 us (93%)
  other arithmetic  8.47 us (4%)
  local copies, waits for them, and re-layouts  4.88 us (2%)
    pallas_call x1, Pallas kernels, give_back(): pl.pallas_call(functools.partial(return_kernel, peers, groups, reach), in...  63 us
    pallas_call x1, Pallas kernels, fetch(): pl.pallas_call(functools.partial(fetch_kernel, peers, groups, reach), in_...  57.5 us
    pallas_call x1, Pallas kernels, finish(): pl.pallas_call(functools.partial(finish_kernel, peers, groups), in_specs=...  37.1 us
    pallas_call x1, Pallas kernels, attention(): pl.pallas_call(attention_kernel, grid_spec=pltpu.PrefetchScalarGridSpec(n...  33.8 us
    pallas_call x1, Pallas kernels, project(): pl.pallas_call(functools.partial(project_kernel, peers, groups), grid=(ro...  16.4 us

profile of v5, /device:TPU:1, one launch (start us, length us, event | category | flops | bytes accessed | tf_op | source)
XLA Modules:
  0.0 223.6 jit_solution(9499939948086483293)
XLA Ops:
  0.6 0.0 copy-start.5
  0.6 16.4 %shard_map.93 = (bf16[1024,1024]{1,0:T(8,128)(2,1)}, bf16[1024,256]{1,0:T(8,128)(2,1)}, bf16[8,4,128,128]{3,2,1,0:T(8,128)(2,1)S(1)}, f32[2,1024]{1,0:T(2,128)}, s32[32,2,32]{2,1,0:T(2,128)}) custom-call(bf16[1024,1024]{1,0:T(8,128)(2,1)} %tokens_ref.3, bf16[3,1024,256]{2,1,0:T(8,128)(2,1)} %bitcast.30, s32[2,32]{1,0:T(2,128)} %bitcast.39), custom_call_target="tpu_custom_call" | custom-call | tf_op jit(solution)/shard_map/pallas_call | solution.py:86
  17.0 0.8 fusion.9
  17.8 0.8 slice_compare_fusion
  18.6 0.6 fusion.8
  20.6 0.9 constant_dynamic-slice_fusion
  21.4 0.1 copy.11
  21.5 0.1 reshape.43
  21.6 0.0 copy-done.5
  21.6 0.0 copy-start.1
  21.6 0.0 copy-start.2
  21.6 0.0 copy-start.4
  21.6 57.5 %conditional.2 = (bf16[4,1024,256]{2,1,0:T(8,128)(2,1)}, bf16[64,4,128,128]{3,2,1,0:T(8,128)(2,1)}) conditional(s32[]{:T(128)} %clamp.4, (s32[64]{0:T(128)S(1)}, bf16[8,4,128,128]{3,2,1,0:T(8,128)(2,1)S(1)}, bf16[1024,256]{1,0:T(8,128)(2,1)S(1)}) %tuple.53, (s32[64]{0:T(128)S(1)}, bf16[8,4,128,128]{3,2,1,0:T(8,128)(2,1)S(1)}, ...), branch_computations={%region_1.2_spmd, %region_2.3_spmd, %region_3.4_spmd} | conditional | bytes 16 | solution.py:639
  21.6 57.5 %branch_0_fun.2 = (bf16[32,2,4,128,128]{4,3,2,1,0:T(8,128)(2,1)}, bf16[4,1024,256]{2,1,0:T(8,128)(2,1)}) custom-call(s32[64]{0:T(128)S(1)} %get-tuple-element.59.wanted_ref, bf16[8,4,128,128]{3,2,1,0:T(8,128)(2,1)S(1)} %get-tuple-element.60.kv_ref, bf16[1024,256]{1,0:T(8,128)(2,1)S(1)} %get-tuple-element.61.cot_ref), custom_call_target="tpu_custom_call" | custom-call | tf_op jit(solution)/shard_map/cond/branch_0_fun/pallas_call | solution.py:225
  79.2 0.0 copy-done.1
  79.2 0.0 copy-done.2
  79.2 0.0 copy-done.4
  79.2 33.8 %shard_map.94 = (bf16[4,1024,256]{2,1,0:T(8,128)(2,1)}, f32[8,4,128,128]{3,2,1,0:T(8,128)}, bf16[64,4,128,128]{3,2,1,0:T(8,128)(2,1)}, bf16[1024,256]{1,0:T(8,128)(2,1)S(1)}, bf16[1024,512]{1,0:T(8,128)(2,1)S(1)}) custom-call(s32[8,9]{1,0:T(8,128)S(1)} %copy-done.4, bf16[1024,256]{1,0:T(8,128)(2,1)S(1)} %copy-done.2, ...), custom_call_target="tpu_custom_call" | custom-call | tf_op jit(solution)/shard_map/pallas_call | solution.py:443
  113.0 0.0 copy-start
  113.0 1.0 copy-done
  114.0 0.0 copy-start.3
  114.0 0.8 copy-done.3
  114.8 65.3 %conditional.3 = (bf16[8,4,128,128]{3,2,1,0:T(8,128)(2,1)S(1)}, f32[1024,256]{1,0:T(8,128)S(1)}) conditional(s32[]{:T(128)} %clamp.4, (bf16[64,4,128,128]{3,2,1,0:T(8,128)(2,1)}, s32[64]{0:T(128)S(1)}, f32[8,4,128,128]{3,2,1,0:T(8,128)}, bf16[4,1024,256]{2,1,0:T(8,128)(2,1)}) %tuple.39, (bf16[64,4,128,128]{3,2,1,0:T(8,128)(2,1)}, ...), branch_computations={%region_4.6_spmd, %region_6.8_spmd, %region_8.10_spmd} | conditional | flops 1835008 | bytes 3145744 | solution.py:653
  114.8 63.0 %branch_0_fun.3 = (bf16[8,4,128,128]{3,2,1,0:T(8,128)(2,1)S(1)}, bf16[4,1024,256]{2,1,0:T(8,128)(2,1)}) custom-call(s32[64]{0:T(128)S(1)} %get-tuple-element.74.wanted_ref, f32[8,4,128,128]{3,2,1,0:T(8,128)} %get-tuple-element.75.near_ref, bf16[32,2,4,128,128]{4,3,2,1,0:T(8,128)(2,1)} %bitcast.3.far_ref, bf16[4,1024,256]{2,1,0:T(8,128)(2,1)} %get-tuple-element.77.att_ref), custom_call_target="tpu_custom_call" | custom-call | tf_op jit(solution)/shard_map/cond/branch_0_fun/pallas_call | solution.py:303
  177.8 2.0 convert_reduce_fusion
  180.0 37.1 %shard_map.95 = (bf16[32,32,512]{2,1,0:T(8,128)(2,1)}, bf16[32,32,512]{2,1,0:T(8,128)(2,1)}, bf16[4,1024,256]{2,1,0:T(8,128)(2,1)}, f32[4,2,1024]{2,1,0:T(2,128)}) custom-call(bf16[1024,1024]{1,0:T(8,128)(2,1)} %tokens_ref.3, bf16[1024,256]{1,0:T(8,128)(2,1)} %copy-done.3, bf16[8,4,128,128]{3,2,1,0:T(8,128)(2,1)S(1)} %get-tuple-element.126.grad_kv_ref, ...), custom_call_target="tpu_custom_call" | custom-call | tf_op jit(solution)/shard_map/pallas_call | solution.py:591
  217.2 0.0 copy-start.8
  217.2 2.0 convert_reduce_fusion.3
  219.2 0.0 copy-done.8
  219.2 0.0 copy-start.6
  219.3 0.0 copy-start.7
  219.3 2.7 %fusion.6 = (bf16[1024,256]{1,0:T(8,128)(2,1)}, bf16[1024,256]{1,0:T(8,128)(2,1)}) fusion(f32[1024,256]{1,0:T(8,128)S(1)} %convert_reduce_fusion.3, bf16[1024,256]{1,0:T(8,128)(2,1)S(1)} %copy-done.5, f32[1024]{0:T(1024)S(1)} %bitcast.37, f32[1024]{0:T(1024)S(1)} %bitcast.35, f32[1024]{0:T(1024)S(1)} %bitcast.36, f32[1024]{0:T(1024)S(1)} %bitcast.34, ...), kind=kLoop, calls=%fused_computation.14 | loop fusion | flops 3145728 | bytes 4210692 | tf_op jit(solution)/shard_map/convert_element_type | solution.py:679
  222.0 0.0 copy-done.6
  222.0 0.0 copy-done.7
  222.0 0.3 convert_reduce_fusion.4
  222.3 0.6 slice_bitcast_fusion
  222.9 0.6 copy.17
  (4 shorter events, 0.0 us)
Async XLA Ops:
  0.6 21.0 %copy-start.5 = (bf16[1024,256]{1,0:T(8,128)(2,1)S(1)}, bf16[1024,256]{1,0:T(8,128)(2,1)}, u32[]{:S(2)}) copy-start(bf16[1024,256]{1,0:T(8,128)(2,1)} %param.17) | copy-start | bytes 1572868
  21.6 57.6 %copy-start.1 = (bf16[256,1024]{1,0:T(8,128)(2,1)S(1)}, bf16[256,1024]{1,0:T(8,128)(2,1)}, u32[]{:S(2)}) copy-start(bf16[256,1024]{1,0:T(8,128)(2,1)} %w_out_ref.1) | copy-start | bytes 1572868
  21.6 57.6 %copy-start.2 = (bf16[1024,256]{1,0:T(8,128)(2,1)S(1)}, bf16[1024,256]{1,0:T(8,128)(2,1)}, u32[]{:S(2)}) copy-start(bf16[1024,256]{1,0:T(8,128)(2,1)} %get-tuple-element.115.q_ref) | copy-start | bytes 1572868
  21.6 57.6 %copy-start.4 = (s32[8,9]{1,0:T(8,128)S(1)}, s32[8,9]{1,0:T(8,128)}, u32[]{:S(2)}) copy-start(s32[8,9]{1,0:T(8,128)} %entries_ref.1) | copy-start | bytes 868
  113.0 1.0 copy-start
  114.0 0.8 copy-start.3
  217.2 2.0 copy-start.8
  219.2 2.7 %copy-start.6 = (bf16[32,32,512]{2,1,0:T(8,128)(2,1)S(1)}, bf16[32,32,512]{2,1,0:T(8,128)(2,1)}, u32[]{:S(2)}) copy-start(bf16[32,32,512]{2,1,0:T(8,128)(2,1)} %get-tuple-element.130) | copy-start | bytes 3145732
  219.3 2.7 %copy-start.7 = (bf16[32,32,512]{2,1,0:T(8,128)(2,1)S(1)}, bf16[32,32,512]{2,1,0:T(8,128)(2,1)}, u32[]{:S(2)}) copy-start(bf16[32,32,512]{2,1,0:T(8,128)(2,1)} %get-tuple-element.131) | copy-start | bytes 3145732
